TPU v7x, 256 devices: a whole 4x4x8 slice. The times are simulated.
256 devices in a mesh: dp: 4 (over z_lo, core), seq: 64 (over z_hi, y, x).
Axes of the slice: x: 4, y: 4, z: 8 (z_hi: 4, z_lo: 2; z = z_hi * 2 + z_lo), core: 2. Of those that a mesh axis runs over, the one named last changes fastest.
Arguments:
- glu_out: bfloat16 [4, 8192, 1536], P('dp', 'seq'), may hold values from -6 to 6
- lengths: int32 [4], replicated, may hold values from 1024 to 8192, as said below
- kernel: float32 [31, 1536], replicated, may hold values from -1 to 1
- gain: float32 [1536], replicated, may hold values from 0.25 to 1.75
- bias: float32 [1536], replicated, may hold values from -3 to 3
- weight: bfloat16 [1536, 1536], P(('dp', 'seq')), may hold values from -0.15625 to 0.15625
- master: float32 [1536, 1536], P(('dp', 'seq')), may hold values from -0.15625 to 0.15625
- moment_one: float32 [1536, 1536], P(('dp', 'seq')), may hold values from -120 to 120
- moment_two: float32 [1536, 1536], P(('dp', 'seq')), may hold values from 100 to 100000
- cotangent: bfloat16 [4, 8192, 1536], P('dp', 'seq'), may hold values from -6 to 6
Outputs:
- module_out: bfloat16 [4, 8192, 1536], P('dp', 'seq')
- input_grad: bfloat16 [4, 8192, 1536], P('dp', 'seq')
- kernel_grad: float32 [31, 1536], replicated
- gain_grad: float32 [1536], replicated
- bias_grad: float32 [1536], replicated
- new_master: float32 [1536, 1536], P(('dp', 'seq'))
- new_one: float32 [1536, 1536], P(('dp', 'seq'))
- new_two: float32 [1536, 1536], P(('dp', 'seq'))
Inputs may be any that keep to these rules, and one draw needn't show every extreme that they name: `lengths`: in every draw one stream has all 8192 frames valid; each other stream has between 1024 and 2730 valid frames.
All inputs are finite; a program needn't handle non-finite values.
Results may differ from a plain program's by a relative error of at most 0.0049.
Values may be sent and summed in bfloat16 or wider, within the bound.
No kernel may reach another device: no remote copies, remote signals or barrier semaphores. Data moves between devices by JAX's collectives and lax.ppermute only.
A program may use at most 64 MiB of HBM per device.

v0:
```python
import jax
import jax.numpy as jnp
from jax import lax
from jax.experimental import pallas as pl
from jax.experimental.pallas import tpu as pltpu
from jax.sharding import Mesh, PartitionSpec as P

KERNEL = 31
HALF = 15
HALO = 32
EDGE = 16

beta_one = 0.9
beta_two = 0.999
adam_rate = 0.001
adam_eps = 1e-08
norm_eps = 1e-05
first_fix = 0.9999734386011124
second_fix = 0.09520785288629043

SEQ = ("zh", "y", "x")
DP = ("zl", "core")
f32 = jnp.float32
bf16 = jnp.bfloat16


def size(axis):
    return lax.axis_size(axis)


def swap(value, axis, mask):
    return lax.ppermute(value, axis, [(i, i ^ mask) for i in range(size(axis))])


def shift(value, axis, step):
    count = size(axis)
    return lax.ppermute(value, axis, [(i, (i + step) % count) for i in range(count)])


def in_order(index, parts):
    odd, high = (index & 1) == 1, (index & 2) == 2
    r0, r1, r2, r3 = parts
    a, b = jnp.where(odd, r1, r0), jnp.where(odd, r0, r1)
    c, d = jnp.where(odd, r3, r2), jnp.where(odd, r2, r3)
    return (jnp.where(high, c, a), jnp.where(high, d, b), jnp.where(high, a, c), jnp.where(high, b, d))


def exchange(value, axis):
    return [value] + [swap(value, axis, m) for m in (1, 2, 3)]


barrier = lax.optimization_barrier
STAGES = (("x", 1), ("x", 2), ("zh", 1), ("zh", 2), ("y", 1), ("y", 2))


def halves(value):
    high = lax.reduce_precision(value, 8, 7)
    low = lax.reduce_precision(value - high, 8, 7)
    cut = value.shape[0] // 2
    parts = [high[:cut], high[cut:], low[:cut], low[cut:]]
    return jnp.concatenate(parts, axis=1).astype(bf16)


def whole_again(rows):
    width = rows.shape[1] // 4
    parts = [rows[:, k * width : (k + 1) * width].astype(f32) for k in range(4)]
    return jnp.concatenate([parts[0] + parts[2], parts[1] + parts[3]], axis=0)


def four(parts):
    return (parts[0] + parts[1]) + (parts[2] + parts[3])


def scatter_stage(value, side, axis, dim):
    me = lax.axis_index(axis)
    width = value.shape[-1]
    packed = halves(side)
    blocks = [lax.dynamic_index_in_dim(value, me ^ m, dim, keepdims=False) for m in range(4)]
    kept, sides = [blocks[0]], [whole_again(packed)]
    for m in (1, 2, 3):
        message = jnp.concatenate([blocks[m].astype(bf16).reshape(-1, width), packed], axis=0)
        message = swap(message, axis, m)
        cut = message.shape[0] - packed.shape[0]
        kept.append(message[:cut].astype(f32).reshape(blocks[0].shape))
        sides.append(whole_again(message[cut:]))
    return four(kept), four(sides)


def combine(stats, axis, mask):
    other = swap(stats, axis, mask)
    n = stats[0:1] + other[0:1]
    mean = (stats[0:1] * stats[1:2] + other[0:1] * other[1:2]) / jnp.maximum(n, 1.0)
    here, there = stats[1:2] - mean, other[1:2] - mean
    spread = stats[2:3] + other[2:3] + stats[0:1] * here * here + other[0:1] * there * there
    return jnp.concatenate([n, mean, spread])


LANES = 128
VMEM_LIMIT = 40 * 1024 * 1024


def valid_in(meta_ref, stream, frames, extra):
    rows = frames + 2 * extra
    place = lax.broadcasted_iota(jnp.int32, (rows, LANES), 0) + (meta_ref[4] * frames - extra)
    return (place >= 0) & (place < meta_ref[stream])


def fold(rows):
    return jnp.sum(rows.reshape(-1, 8, LANES), axis=0)


def squash(rows):
    return jnp.sum(rows, axis=0, keepdims=True)


def conv_kernel(meta_ref, slab_ref, taps_ref, masked_ref, conv_ref, stats_ref):
    span = conv_ref.shape[1]
    frames = span - 2 * EDGE
    half = span // 2
    n = jnp.int32(0)
    total = jnp.zeros((8, LANES), f32)
    for s in range(4):
        n = n + jnp.clip(meta_ref[s] - meta_ref[4] * frames, 0, frames)
        slab = slab_ref[s].astype(f32)
        masked_ref[s] = jnp.where(valid_in(meta_ref, s, frames, HALO), slab, 0.0)
        for part in range(2):
            acc = jnp.zeros((half, LANES), f32)
            for tap in range(KERNEL):
                begin = HALO - EDGE - HALF + tap + part * half
                acc = acc + taps_ref[tap : tap + 1, :] * masked_ref[s, begin : begin + half, :]
            conv_ref[s, part * half : (part + 1) * half, :] = acc
        inner = conv_ref[s, EDGE : EDGE + frames, :]
        total = total + fold(jnp.where(valid_in(meta_ref, s, frames, 0), inner, 0.0))
    number = jnp.full((1, LANES), n, jnp.int32).astype(f32)
    mean = squash(total) / jnp.maximum(number, 1.0)
    spread = jnp.zeros((8, LANES), f32)
    for s in range(4):
        off = conv_ref[s, EDGE : EDGE + frames, :] - mean
        off = jnp.where(valid_in(meta_ref, s, frames, 0), off, 0.0)
        spread = spread + fold(off * off)
    stats_ref[0:1, :] = number
    stats_ref[1:2, :] = mean
    stats_ref[2:3, :] = squash(spread)


def moment_kernel(meta_ref, masked_ref, conv_ref, mean_ref, in_ref, off_ref, ones, offs):
    frames = ones.shape[1]
    for s in range(4):
        valid = valid_in(meta_ref, s, frames, 0)
        ones[s] = jnp.where(valid, 1.0, 0.0)
        offs[s] = jnp.where(valid, conv_ref[s, EDGE : EDGE + frames, :] - mean_ref[...], 0.0)
    for tap in range(KERNEL):
        begin = HALO - HALF + tap
        plain, centred = jnp.zeros((8, LANES), f32), jnp.zeros((8, LANES), f32)
        for s in range(4):
            moved = masked_ref[s, begin : begin + frames, :]
            plain = plain + fold(ones[s] * moved)
            centred = centred + fold(offs[s] * moved)
        in_ref[tap : tap + 1, :] = squash(plain)
        off_ref[tap : tap + 1, :] = squash(centred)


def gate_kernel(meta_ref, conv_ref, back_ref, masked_ref, stats_ref, affine_ref, hidden_ref, grad_ref, sums_ref):
    count = jnp.full((1, LANES), meta_ref[5], jnp.int32).astype(f32)
    inv_std = lax.rsqrt(stats_ref[2:3, :] / count + norm_eps)
    span = conv_ref.shape[1]
    frames = span - 2 * EDGE
    gain_sum, bias_sum = jnp.zeros((8, LANES), f32), jnp.zeros((8, LANES), f32)
    for s in range(4):
        standard = (conv_ref[s] - stats_ref[1:2, :]) * inv_std
        scaled = affine_ref[0:1, :] * standard + affine_ref[1:2, :]
        logistic = jax.nn.sigmoid(scaled)
        hidden = scaled * logistic
        hidden_ref[s] = hidden[EDGE : EDGE + frames].astype(bf16)
        grad = back_ref[s] * logistic * (1.0 + scaled * (1.0 - logistic))
        grad_ref[s] = grad
        inner = grad[EDGE : EDGE + frames]
        gain_sum = gain_sum + fold(inner * standard[EDGE : EDGE + frames])
        bias_sum = bias_sum + fold(inner)
    for tap in range(KERNEL):
        begin = HALO - HALF + tap
        acc = jnp.zeros((8, LANES), f32)
        for s in range(4):
            acc = acc + fold(grad_ref[s, EDGE : EDGE + frames, :] * masked_ref[s, begin : begin + frames, :])
        sums_ref[tap : tap + 1, :] = squash(acc)
    sums_ref[KERNEL : KERNEL + 1, :] = squash(gain_sum)
    sums_ref[KERNEL + 1 : KERNEL + 2, :] = squash(bias_sum)
    sums_ref[KERNEL + 2 : KERNEL + 3, :] = jnp.zeros((1, LANES), f32)


def input_kernel(meta_ref, conv_ref, grad_ref, stats_ref, affine_ref, sums_ref, taps_ref, out_ref, back):
    span = conv_ref.shape[1]
    frames = span - 2 * EDGE
    count = jnp.full((1, LANES), meta_ref[5], jnp.int32).astype(f32)
    inv_std = lax.rsqrt(stats_ref[2:3, :] / count + norm_eps)
    gain = affine_ref[0:1, :]
    gain_part = gain * sums_ref[KERNEL : KERNEL + 1, :] / count
    bias_part = gain * sums_ref[KERNEL + 1 : KERNEL + 2, :] / count
    for s in range(4):
        standard = (conv_ref[s] - stats_ref[1:2, :]) * inv_std
        grad = inv_std * (gain * grad_ref[s] - bias_part - standard * gain_part)
        back[s] = jnp.where(valid_in(meta_ref, s, frames, EDGE), grad, 0.0)
        valid = valid_in(meta_ref, s, frames, 0)
        half = frames // 2
        for part in range(2):
            acc = jnp.zeros((half, LANES), f32)
            for tap in range(KERNEL):
                begin = EDGE + HALF - tap + part * half
                acc = acc + taps_ref[tap : tap + 1, :] * back[s, begin : begin + half, :]
            rows = slice(part * half, (part + 1) * half)
            out_ref[s, rows, :] = jnp.where(valid[rows], acc, 0.0).astype(bf16)


def by_lanes(kernel, ins, outs, scratch=(), meta=None):
    def spec(array):
        lead = array.shape[:-1]
        return pl.BlockSpec(lead + (LANES,), lambda i, *_: (0,) * len(lead) + (i,))

    shapes = [jax.ShapeDtypeStruct(shape, dtype) for shape, dtype in outs]
    prefetch = [] if meta is None else [meta]
    return pl.pallas_call(
        kernel,
        out_shape=shapes,
        grid_spec=pltpu.PrefetchScalarGridSpec(
            num_scalar_prefetch=len(prefetch),
            grid=(ins[0].shape[-1] // LANES,),
            in_specs=[spec(x) for x in ins],
            out_specs=[spec(x) for x in shapes],
            scratch_shapes=list(scratch),
        ),
        compiler_params=pltpu.CompilerParams(vmem_limit_bytes=VMEM_LIMIT),
    )(*prefetch, *ins)


def on_device(
    glu_out, lengths, kernel, gain, bias, weight, master, moment_one, moment_two, cotangent
):
    frames, width = glu_out.shape[1:]
    dp = lax.axis_index(DP)
    seq = lax.axis_index(SEQ)
    own = width // 4

    glu_out, cotangent = glu_out[0], cotangent[0]
    below = jnp.concatenate([glu_out[frames - HALO :], cotangent[frames - EDGE :]])
    above = jnp.concatenate([glu_out[:HALO], cotangent[:EDGE]])
    below, above, weight = barrier((below, above, weight))
    low, high = shift(below, SEQ, 1), shift(above, SEQ, -1)
    rows = exchange(weight, "x")
    low, high, rows, lengths, kernel, gain, bias = barrier(
        (low, high, rows, lengths, kernel, gain, bias)
    )
    cot = jnp.concatenate([low[HALO:], cotangent, high[HALO:]], axis=0)
    cot_z = swap(cot, "zl", 1)
    slab = jnp.concatenate([low[:HALO], glu_out, high[:HALO]], axis=0)
    pick = lambda m: lax.dynamic_slice_in_dim(slab, (dp ^ m) * own, own, axis=1)
    pieces = [pick(0)] + [swap(pick(m), DP, m) for m in (1, 2, 3)]
    total = jnp.sum(lengths)
    count = total.astype(f32)
    places = jnp.arange(4, dtype=jnp.int32)
    limit = jnp.sum(jnp.where(places[None, :] == (dp ^ places)[:, None], lengths, 0), axis=1)
    meta = jnp.concatenate([limit, jnp.stack([seq, total])])

    rows, pieces[2] = barrier((rows, pieces[2]))
    rows = jnp.concatenate(in_order(lax.axis_index("x"), rows), axis=0)
    rows = jnp.stack(in_order(lax.axis_index("zh"), exchange(rows, "zh")), axis=0)
    slabs = jnp.stack(pieces)
    slabs, meta = barrier((slabs, meta))

    def valid_rows(extra):
        positions = seq * frames - extra + jnp.arange(frames + 2 * extra, dtype=jnp.int32)
        return ((positions >= 0) & (positions < limit[:, None]))[:, :, None]

    def mine(table):
        return lax.dynamic_slice_in_dim(table, dp * own, own, axis=table.ndim - 1)

    taps, affine = mine(kernel), mine(jnp.stack([gain, bias]))
    gain_own = affine[0:1]

    span = frames + 2 * EDGE
    masked, conv_out, stats = by_lanes(
        conv_kernel,
        [slabs, taps],
        [((4, frames + 2 * HALO, own), f32), ((4, span, own), f32), ((3, own), f32)],
        meta=meta,
    )
    mean = stats[1:2]
    stats, cot_z, affine = barrier((stats, cot_z, affine))

    pair = swap(jnp.stack([cot, cot_z]), "core", 1)
    stats = combine(stats, *STAGES[0])
    stats, rows, mean, pair = barrier((stats, rows, mean, pair))
    rows = jnp.stack(in_order(lax.axis_index("y"), exchange(rows, "y")), axis=1).reshape(own, width)
    grad_out = jnp.stack([cot, pair[0], cot_z, pair[1]])
    grad_out = jnp.where(valid_rows(EDGE), grad_out, jnp.zeros((), bf16))
    hidden_grad = lax.dot_general(
        grad_out.reshape(4 * span, width), rows, (((1,), (1,)), ((), ())), preferred_element_type=f32
    ).reshape(4, span, own)

    tap_in, tap_off = by_lanes(
        moment_kernel,
        [masked, conv_out, mean],
        [((KERNEL, own), f32)] * 2,
        [pltpu.VMEM((4, frames, LANES), f32)] * 2,
        meta=meta,
    )
    for axis, mask in STAGES[1:4]:
        stats = combine(stats, axis, mask)
    grad_inner = grad_out[:, EDGE : EDGE + frames].reshape(4 * frames, width)
    stats, hidden_grad, tap_in, tap_off, grad_inner = barrier(
        (stats, hidden_grad, tap_in, tap_off, grad_inner)
    )
    for axis, mask in STAGES[4:]:
        stats = combine(stats, axis, mask)

    hidden, scaled_grad, sums = by_lanes(
        gate_kernel,
        [conv_out, hidden_grad, masked, stats, affine],
        [((4, frames, own), bf16), ((4, span, own), f32), ((KERNEL + 3, own), f32)],
        meta=meta,
    )
    stats, tap_in, tap_off, sums = barrier((stats, tap_in, tap_off, sums))
    channel_mean = stats[1:2]
    inv_std = lax.rsqrt(stats[2:3] / count + norm_eps)
    tap_pair = jnp.stack([tap_in, inv_std * (tap_off + (mean - channel_mean) * tap_in)])

    flat = hidden.reshape(4 * frames, own)
    weight_grad = lax.dot_general(
        flat,
        grad_inner,
        (((0,), (0,)), ((), ())),
        preferred_element_type=f32,
    ).reshape(4, 4, own // 16, width)
    product = jnp.dot(flat, rows, preferred_element_type=f32).reshape(4, frames, width)

    weight_grad, sums = scatter_stage(weight_grad, sums, "y", 1)
    other = swap(jnp.stack([product[1], product[3]]).astype(bf16), "core", 1).astype(f32)
    kept, far = product[0] + other[0], product[2] + other[1]
    product = kept + swap(far.astype(bf16), "zl", 1).astype(f32)
    for axis, mask in STAGES[:3]:
        tap_pair = tap_pair + swap(tap_pair, axis, mask)
    weight_grad, sums, tap_pair, product = barrier((weight_grad, sums, tap_pair, product))
    weight_grad, sums = scatter_stage(weight_grad, sums, "zh", 0)
    for axis, mask in STAGES[4:]:
        tap_pair = tap_pair + swap(tap_pair, axis, mask)
    weight_grad, sums, tap_pair = barrier((weight_grad, sums, tap_pair))
    weight_grad, sums = scatter_stage(weight_grad.reshape(4, own // 64, width), sums, "x", 0)
    for axis, mask in STAGES[3:4]:
        tap_pair = tap_pair + swap(tap_pair, axis, mask)
    stream_valid = (seq * frames + jnp.arange(frames, dtype=jnp.int32) < limit[0])[:, None]
    module_out = jnp.where(stream_valid, product, 0.0).astype(bf16)

    (flipped,) = by_lanes(
        input_kernel,
        [conv_out, scaled_grad, stats, affine, sums, taps],
        [((4, frames, own), bf16)],
        [pltpu.VMEM((4, span, LANES), f32)],
        meta=meta,
    )
    _, sums = barrier((flipped, sums))
    gain_grad, bias_grad = sums[KERNEL : KERNEL + 1], sums[KERNEL + 1 : KERNEL + 2]
    tap_sums = (inv_std * gain_own) * (
        sums[:KERNEL] - bias_grad / count * tap_pair[0] - gain_grad / count * tap_pair[1]
    )
    table = jnp.concatenate([tap_sums, sums[KERNEL : KERNEL + 2]], axis=0)
    parts = [flipped[0]] + [swap(flipped[m], DP, m) for m in (1, 2, 3)]
    input_grad = jnp.concatenate(in_order(dp, parts), axis=1)
    table = jnp.concatenate(in_order(dp, exchange(table, DP)), axis=1)

    new_one = beta_one * moment_one + (1.0 - beta_one) * weight_grad
    new_two = beta_two * moment_two + (1.0 - beta_two) * weight_grad * weight_grad
    new_master = master - adam_rate * (new_one / first_fix) / (
        jnp.sqrt(new_two / second_fix) + adam_eps
    )
    return (
        module_out[None],
        input_grad[None],
        table[:KERNEL],
        table[KERNEL],
        table[KERNEL + 1],
        new_master,
        new_one,
        new_two,
    )


def solution(mesh):
    fine = Mesh(mesh.devices.reshape(2, 2, 4, 4, 4), DP + SEQ)
    whole, split, tall = P(), P(DP, SEQ, None), P(DP + SEQ, None)
    return jax.shard_map(
        on_device,
        mesh=fine,
        in_specs=(split, whole, whole, whole, whole, tall, tall, tall, tall, split),
        out_specs=(split, split, whole, whole, whole, tall, tall, tall),
        check_vma=False,
    )
```

profile of v0, /device:TPU:1, one launch (start us, length us, event | category | flops | bytes accessed | tf_op | source)
XLA Modules:
  0.0 171.9 jit_solution(2713210987998512819)
XLA Ops:
  2.6 2.1 %collective-permute-start.2 = (bf16[6,1536]{1,0:T(8,128)(2,1)}, bf16[6,1536]{1,0:T(8,128)(2,1)S(1)}, u32[]{:S(2)}, u32[]{:S(2)}) collective-permute-start(bf16[6,1536]{1,0:T(8,128)(2,1)} %param.15), channel_id=1, source_target_pairs={{0,1},{1,0},{2,3},{3,2},{4,5},{5,4},{6,7},{7,6},{8,9},{9,8},{10,11... | collective-permute-start | bytes 55304 | tf_op jit(solution)/shard_map/ppermute | solution.py:32
  4.7 2.5 %collective-permute-start.3 = (bf16[6,1536]{1,0:T(8,128)(2,1)}, bf16[6,1536]{1,0:T(8,128)(2,1)S(1)}, u32[]{:S(2)}, u32[]{:S(2)}) collective-permute-start(bf16[6,1536]{1,0:T(8,128)(2,1)} %param.15), channel_id=1, source_target_pairs={{0,2},{1,3},{2,0},{3,1},{4,6},{5,7},{6,4},{7,5},{8,10},{9,11},{10,... | collective-permute-start | bytes 55304 | tf_op jit(solution)/shard_map/ppermute | solution.py:32
  7.3 10.7 %collective-permute-start.1 = (bf16[48,1536]{1,0:T(8,128)(2,1)S(1)}, bf16[48,1536]{1,0:T(8,128)(2,1)S(1)}, u32[]{:S(2)}, u32[]{:S(2)}) collective-permute-start(bf16[48,1536]{1,0:T(8,128)(2,1)S(1)} %get-tuple-element.61), channel_id=1, source_target_pairs={{0,63},{1,0},{2,1},{3,2},{4,3},{5,4},{6,5},{7,6},{8,7},{9,8},{10,9... | collective-permute-start | bytes 442376 | tf_op jit(solution)/shard_map/ppermute | solution.py:37
  18.1 3.6 %collective-permute-done = bf16[48,1536]{1,0:T(8,128)(2,1)S(1)} collective-permute-done((bf16[48,1536]{1,0:T(8,128)(2,1)S(1)}, bf16[48,1536]{1,0:T(8,128)(2,1)S(1)}, u32[]{:S(2)}, u32[]{:S(2)}) %collective-permute-start) | collective-permute-done | bytes 147488 | tf_op jit(solution)/shard_map/ppermute | solution.py:37
  21.7 1.9 %collective-permute-done.1 = bf16[48,1536]{1,0:T(8,128)(2,1)S(1)} collective-permute-done((bf16[48,1536]{1,0:T(8,128)(2,1)S(1)}, bf16[48,1536]{1,0:T(8,128)(2,1)S(1)}, u32[]{:S(2)}, u32[]{:S(2)}) %collective-permute-start.1) | collective-permute-done | bytes 147488 | tf_op jit(solution)/shard_map/ppermute | solution.py:37
  23.8 3.1 %collective-permute-start.7 = (bf16[192,384]{1,0:T(8,128)(2,1)S(1)}, bf16[192,384]{1,0:T(8,128)(2,1)S(1)}, u32[]{:S(2)}, u32[]{:S(2)}) collective-permute-start(bf16[192,384]{1,0:T(8,128)(2,1)S(1)} %get-tuple-element.156), channel_id=1, source_target_pairs={{0,192},{64,128},{128,64},{192,0},{1,193},{65,129},{129,65},{193,1... | collective-permute-start | bytes 442376 | tf_op jit(solution)/shard_map/ppermute | solution.py:32
  30.2 4.0 %collective-permute-done.6 = bf16[192,384]{1,0:T(8,128)(2,1)S(1)} collective-permute-done((bf16[192,384]{1,0:T(8,128)(2,1)S(1)}, bf16[192,384]{1,0:T(8,128)(2,1)S(1)}, u32[]{:S(2)}, u32[]{:S(2)}) %collective-permute-start.6) | collective-permute-done | bytes 147488 | tf_op jit(solution)/shard_map/ppermute | solution.py:32
  34.3 3.0 %collective-permute-start.10 = (bf16[24,1536]{1,0:T(8,128)(2,1)S(1)}, bf16[24,1536]{1,0:T(8,128)(2,1)S(1)}, u32[]{:S(2)}, u32[]{:S(2)}) collective-permute-start(bf16[24,1536]{1,0:T(8,128)(2,1)S(1)} %pad_maximum_fusion.19), channel_id=1, source_target_pairs={{0,48},{16,32},{32,16},{48,0},{1,49},{17,33},{33,17},{49,1},{2,50}... | collective-permute-start | bytes 221192 | tf_op jit(solution)/shard_map/ppermute | solution.py:32
  40.1 3.5 %shard_map.161 = (f32[4,192,384]{2,1,0:T(8,128)S(1)}, f32[4,160,384]{2,1,0:T(8,128)S(1)}, f32[3,384]{1,0:T(4,128)S(1)}) custom-call(s32[6]{0:T(128)S(1)} %pad_add_fusion.meta_ref, bf16[4,192,384]{2,1,0:T(8,128)(2,1)S(1)} %pad_maximum_fusion.4.slab_ref, f32[31,384]{1,0:T(8,128)S(1)} %constant_dynamic-slice_fusion.taps_ref), custom_call_target="tpu_custom_call" | custom-call | tf_op jit(solution)/shard_map/pallas_call | solution.py:221
  43.6 2.9 %collective-permute-done.8 = bf16[160,1536]{1,0:T(8,128)(2,1)S(1)} collective-permute-done((bf16[160,1536]{1,0:T(8,128)(2,1)S(1)}, bf16[160,1536]{1,0:T(8,128)(2,1)S(1)}, u32[]{:S(2)}, u32[]{:S(2)}) %collective-permute-start.8) | collective-permute-done | bytes 491552 | tf_op jit(solution)/shard_map/ppermute | solution.py:32
  46.6 2.0 %collective-permute-start.13 = (bf16[2,160,1536]{2,1,0:T(8,128)(2,1)S(1)}, bf16[2,160,1536]{2,1,0:T(8,128)(2,1)S(1)}, u32[]{:S(2)}, u32[]{:S(2)}) collective-permute-start(bf16[2,160,1536]{2,1,0:T(8,128)(2,1)S(1)} %pad_maximum_fusion.1), channel_id=1, source_target_pairs={{0,64},{64,0},{1,65},{65,1},{2,66},{66,2},{3,67},{67,3},{4,68},{68... | collective-permute-start | bytes 2949128 | tf_op jit(solution)/shard_map/ppermute | solution.py:32
  48.6 2.5 %collective-permute-done.10 = bf16[24,1536]{1,0:T(8,128)(2,1)S(1)} collective-permute-done((bf16[24,1536]{1,0:T(8,128)(2,1)S(1)}, bf16[24,1536]{1,0:T(8,128)(2,1)S(1)}, u32[]{:S(2)}, u32[]{:S(2)}) %collective-permute-start.10) | collective-permute-done | bytes 73760 | tf_op jit(solution)/shard_map/ppermute | solution.py:32
  51.9 2.4 %collective-permute-done.9 = f32[3,384]{1,0:T(4,128)S(1)} collective-permute-done((f32[3,384]{1,0:T(4,128)S(1)}, f32[3,384]{1,0:T(4,128)S(1)}, u32[]{:S(2)}, u32[]{:S(2)}) %collective-permute-start.9) | collective-permute-done | bytes 4640 | tf_op jit(solution)/shard_map/ppermute | solution.py:32
  54.5 3.8 %collective-permute-start.17 = (bf16[4,24,1536]{2,1,0:T(8,128)(2,1)S(1)}, bf16[4,24,1536]{2,1,0:T(8,128)(2,1)S(1)}, u32[]{:S(2)}, u32[]{:S(2)}) collective-permute-start(bf16[4,24,1536]{2,1,0:T(8,128)(2,1)S(1)} %pad_maximum_fusion.10), channel_id=1, source_target_pairs={{0,12},{4,8},{8,4},{12,0},{1,13},{5,9},{9,5},{13,1},{2,14},{6,10},... | collective-permute-start | bytes 884744 | tf_op jit(solution)/shard_map/ppermute | solution.py:32
  59.0 3.6 %collective-permute-start.15 = (f32[3,384]{1,0:T(4,128)S(1)}, f32[3,384]{1,0:T(4,128)S(1)}, u32[]{:S(2)}, u32[]{:S(2)}) collective-permute-start(f32[3,384]{1,0:T(4,128)S(1)} %pad_maximum_fusion.26), channel_id=1, source_target_pairs={{0,16},{16,0},{32,48},{48,32},{1,17},{17,1},{33,49},{49,33},{2,18}... | collective-permute-start | bytes 13832 | tf_op jit(solution)/shard_map/ppermute | solution.py:32
  63.6 6.3 %collective-permute-start.16 = (f32[3,384]{1,0:T(4,128)S(1)}, f32[3,384]{1,0:T(4,128)S(1)}, u32[]{:S(2)}, u32[]{:S(2)}) collective-permute-start(f32[3,384]{1,0:T(4,128)S(1)} %pad_maximum_fusion.27), channel_id=1, source_target_pairs={{0,32},{16,48},{32,0},{48,16},{1,33},{17,49},{33,1},{49,17},{2,34}... | collective-permute-start | bytes 13832 | tf_op jit(solution)/shard_map/ppermute | solution.py:32
  71.5 4.9 %shard_map.162 = (f32[31,384]{1,0:T(8,128)S(1)}, f32[31,384]{1,0:T(8,128)S(1)}) custom-call(s32[6]{0:T(128)S(1)} %pad_add_fusion.meta_ref, f32[4,192,384]{2,1,0:T(8,128)S(1)} %get-tuple-element.87.masked_ref, f32[4,160,384]{2,1,0:T(8,128)S(1)} %get-tuple-element.74.conv_ref, f32[1,384]{1,0:T(1,128)S(1)} %slice.494.mean_ref), custom_call_target="tpu_custom_call" | custom-call | tf_op jit(solution)/shard_map/pallas_call | solution.py:221
  76.9 2.2 %fusion.56.back_ref = f32[4,160,384]{2,1,0:T(8,128)} fusion(bf16[4,160,1536]{2,1,0:T(8,128)(2,1)S(1)} %maximum_select_fusion, bf16[384,1536,1]{1,0,2:T(8,128)(2,1)S(1)} %bitcast.155), kind=kOutput, calls=%fused_computation.248 | convolution fusion | flops 754974720 | bytes 4128768 | tf_op jit(solution)/shard_map/dot_general | solution.py:295
  81.6 2.5 %collective-permute-start.21 = (f32[3,384]{1,0:T(4,128)S(1)}, f32[3,384]{1,0:T(4,128)S(1)}, u32[]{:S(2)}, u32[]{:S(2)}) collective-permute-start(f32[3,384]{1,0:T(4,128)S(1)} %pad_maximum_fusion.29), channel_id=1, source_target_pairs={{0,8},{4,12},{8,0},{12,4},{1,9},{5,13},{9,1},{13,5},{2,10},{6,14},... | collective-permute-start | bytes 13832 | tf_op jit(solution)/shard_map/ppermute | solution.py:32
  86.9 3.5 %shard_map.163 = (bf16[4,128,384]{2,1,0:T(8,128)(2,1)S(1)}, f32[4,160,384]{2,1,0:T(8,128)S(1)}, f32[34,384]{1,0:T(8,128)S(1)}) custom-call(s32[6]{0:T(128)S(1)} %pad_add_fusion.meta_ref, f32[4,160,384]{2,1,0:T(8,128)S(1)} %get-tuple-element.74.conv_ref, f32[4,160,384]{2,1,0:T(8,128)S(1)} %copy-done.3, f32[4,192,384]{2,1,0:T(8,128)S(1)} %get-tuple-element.87.masked_ref, ...), custom_call_target="tpu_custom_call" | custom-call | tf_op jit(solution)/shard_map/pallas_call | solution.py:221
  91.6 2.2 %fusion = f32[4,4,24,1536]{3,2,1,0:T(8,128)S(1)} fusion(bf16[4,4,24,512]{3,2,1,0:T(8,128)(2,1)S(1)} %bitcast.160, bf16[512,1536]{1,0:T(8,128)(2,1)} %bitcast.154), kind=kOutput, calls=%fused_computation.1 | convolution fusion | flops 603979776 | bytes 4325376 | tf_op jit(solution)/shard_map/dot_general | solution.py:327
  94.0 2.5 %collective-permute-start.23 = (bf16[113,1536]{1,0:T(8,128)(2,1)S(1)}, bf16[113,1536]{1,0:T(8,128)(2,1)S(1)}, u32[]{:S(2)}, u32[]{:S(2)}) collective-permute-start(bf16[113,1536]{1,0:T(8,128)(2,1)S(1)} %get-tuple-element.209), channel_id=1, source_target_pairs={{0,8},{4,12},{8,0},{12,4},{1,9},{5,13},{9,1},{13,5},{2,10},{6,14},... | collective-permute-start | bytes 1041416 | tf_op jit(solution)/shard_map/ppermute | solution.py:32
  101.8 4.5 %collective-permute-done.26 = f32[2,31,384]{2,1,0:T(8,128)S(1)} collective-permute-done((f32[2,31,384]{2,1,0:T(8,128)S(1)}, f32[2,31,384]{2,1,0:T(8,128)S(1)}, u32[]{:S(2)}, u32[]{:S(2)}) %collective-permute-start.26) | collective-permute-done | bytes 95264 | tf_op jit(solution)/shard_map/ppermute | solution.py:32
  106.4 2.4 %collective-permute-start.27 = (f32[2,31,384]{2,1,0:T(8,128)S(1)}, f32[2,31,384]{2,1,0:T(8,128)S(1)}, u32[]{:S(2)}, u32[]{:S(2)}) collective-permute-start(f32[2,31,384]{2,1,0:T(8,128)S(1)} %fusion.62), channel_id=1, source_target_pairs={{0,16},{16,0},{32,48},{48,32},{1,17},{17,1},{33,49},{49,33},{2,18}... | collective-permute-start | bytes 285704 | tf_op jit(solution)/shard_map/ppermute | solution.py:32
  108.9 9.0 %collective-permute-start.28 = (bf16[2,128,1536]{2,1,0:T(8,128)(2,1)S(1)}, bf16[2,128,1536]{2,1,0:T(8,128)(2,1)S(1)}, u32[]{:S(2)}, u32[]{:S(2)}) collective-permute-start(bf16[2,128,1536]{2,1,0:T(8,128)(2,1)S(1)} %pad_maximum_fusion.2), channel_id=1, source_target_pairs={{0,64},{64,0},{1,65},{65,1},{2,66},{66,2},{3,67},{67,3},{4,68},{68... | collective-permute-start | bytes 2359304 | tf_op jit(solution)/shard_map/ppermute | solution.py:32
  121.0 8.9 %collective-permute-done.29 = bf16[128,1536]{1,0:T(8,128)(2,1)S(1)} collective-permute-done((bf16[128,1536]{1,0:T(8,128)(2,1)S(1)}, bf16[128,1536]{1,0:T(8,128)(2,1)S(1)}, u32[]{:S(2)}, u32[]{:S(2)}) %collective-permute-start.29) | collective-permute-done | bytes 393248 | tf_op jit(solution)/shard_map/ppermute | solution.py:32
  132.6 4.7 %collective-permute-start.31 = (bf16[41,1536]{1,0:T(8,128)(2,1)S(1)}, bf16[41,1536]{1,0:T(8,128)(2,1)S(1)}, u32[]{:S(2)}, u32[]{:S(2)}) collective-permute-start(bf16[41,1536]{1,0:T(8,128)(2,1)S(1)} %get-tuple-element.205), channel_id=1, source_target_pairs={{0,32},{16,48},{32,0},{48,16},{1,33},{17,49},{33,1},{49,17},{2,34}... | collective-permute-start | bytes 377864 | tf_op jit(solution)/shard_map/ppermute | solution.py:32
  138.0 5.5 %collective-permute-done.30 = bf16[41,1536]{1,0:T(8,128)(2,1)S(1)} collective-permute-done((bf16[41,1536]{1,0:T(8,128)(2,1)S(1)}, bf16[41,1536]{1,0:T(8,128)(2,1)S(1)}, u32[]{:S(2)}, u32[]{:S(2)}) %collective-permute-start.30) | collective-permute-done | bytes 125984 | tf_op jit(solution)/shard_map/ppermute | solution.py:32
  148.4 5.0 %collective-permute-start.41 = (f32[2,31,384]{2,1,0:T(8,128)S(1)}, f32[2,31,384]{2,1,0:T(8,128)S(1)}, u32[]{:S(2)}, u32[]{:S(2)}) collective-permute-start(f32[2,31,384]{2,1,0:T(8,128)S(1)} %add.441), channel_id=1, source_target_pairs={{0,32},{16,48},{32,0},{48,16},{1,33},{17,49},{33,1},{49,17},{2,34}... | collective-permute-start | bytes 285704 | tf_op jit(solution)/shard_map/ppermute | solution.py:32
  153.5 3.0 %shard_map.164 = bf16[4,128,384]{2,1,0:T(8,128)(2,1)S(1)} custom-call(s32[6]{0:T(128)S(1)} %pad_add_fusion.meta_ref, f32[4,160,384]{2,1,0:T(8,128)S(1)} %get-tuple-element.74.conv_ref, f32[4,160,384]{2,1,0:T(8,128)S(1)} %copy-done.2, f32[3,384]{1,0:T(4,128)S(1)} %pad_maximum_fusion.30.stats_ref, f32[2,384]{1,0:T(2,128)S(1)} %fusion.31.affine_ref, ...), custom_call_target="tpu_custom_call" | custom-call | tf_op jit(solution)/shard_map/pallas_call | solution.py:221
  156.6 5.9 %collective-permute-start.38 = (bf16[128,384]{1,0:T(8,128)(2,1)S(1)}, bf16[128,384]{1,0:T(8,128)(2,1)S(1)}, u32[]{:S(2)}, u32[]{:S(2)}) collective-permute-start(bf16[128,384]{1,0:T(8,128)(2,1)S(1)} %get-tuple-element.163), channel_id=1, source_target_pairs={{0,192},{64,128},{128,64},{192,0},{1,193},{65,129},{129,65},{193,1... | collective-permute-start | bytes 294920 | tf_op jit(solution)/shard_map/ppermute | solution.py:32
  165.5 2.9 %collective-permute-done.42 = f32[33,384]{1,0:T(8,128)S(1)} collective-permute-done((f32[33,384]{1,0:T(8,128)S(1)}, f32[33,384]{1,0:T(8,128)S(1)}, u32[]{:S(2)}, u32[]{:S(2)}) %collective-permute-start.42) | collective-permute-done | bytes 50720 | tf_op jit(solution)/shard_map/ppermute | solution.py:32
  (209 shorter events, 42.6 us)
Async XLA Ops:
  2.6 15.5 %collective-permute-start.2 = (bf16[6,1536]{1,0:T(8,128)(2,1)}, bf16[6,1536]{1,0:T(8,128)(2,1)S(1)}, u32[]{:S(2)}, u32[]{:S(2)}) collective-permute-start(bf16[6,1536]{1,0:T(8,128)(2,1)} %param.15), channel_id=1, source_target_pairs={{0,1},{1,0},{2,3},{3,2},{4,5},{5,4},{6,7},{7,6},{8,9},{9,8},{10,11... | collective-permute-start | bytes 55304 | tf_op jit(solution)/shard_map/ppermute | solution.py:32
  4.7 13.4 %collective-permute-start.3 = (bf16[6,1536]{1,0:T(8,128)(2,1)}, bf16[6,1536]{1,0:T(8,128)(2,1)S(1)}, u32[]{:S(2)}, u32[]{:S(2)}) collective-permute-start(bf16[6,1536]{1,0:T(8,128)(2,1)} %param.15), channel_id=1, source_target_pairs={{0,2},{1,3},{2,0},{3,1},{4,6},{5,7},{6,4},{7,5},{8,10},{9,11},{10,... | collective-permute-start | bytes 55304 | tf_op jit(solution)/shard_map/ppermute | solution.py:32
  7.1 11.0 %collective-permute-start.4 = (bf16[6,1536]{1,0:T(8,128)(2,1)}, bf16[6,1536]{1,0:T(8,128)(2,1)S(1)}, u32[]{:S(2)}, u32[]{:S(2)}) collective-permute-start(bf16[6,1536]{1,0:T(8,128)(2,1)} %param.15), channel_id=1, source_target_pairs={{0,3},{1,2},{2,1},{3,0},{4,7},{5,6},{6,5},{7,4},{8,11},{9,10},{10,... | collective-permute-start | bytes 55304 | tf_op jit(solution)/shard_map/ppermute | solution.py:32
  7.2 14.5 %collective-permute-start = (bf16[48,1536]{1,0:T(8,128)(2,1)S(1)}, bf16[48,1536]{1,0:T(8,128)(2,1)S(1)}, u32[]{:S(2)}, u32[]{:S(2)}) collective-permute-start(bf16[48,1536]{1,0:T(8,128)(2,1)S(1)} %get-tuple-element.60), channel_id=1, source_target_pairs={{0,1},{1,2},{2,3},{3,4},{4,5},{5,6},{6,7},{7,8},{8,9},{9,10},{10,1... | collective-permute-start | bytes 442376 | tf_op jit(solution)/shard_map/ppermute | solution.py:37
  7.3 16.2 %collective-permute-start.1 = (bf16[48,1536]{1,0:T(8,128)(2,1)S(1)}, bf16[48,1536]{1,0:T(8,128)(2,1)S(1)}, u32[]{:S(2)}, u32[]{:S(2)}) collective-permute-start(bf16[48,1536]{1,0:T(8,128)(2,1)S(1)} %get-tuple-element.61), channel_id=1, source_target_pairs={{0,63},{1,0},{2,1},{3,2},{4,3},{5,4},{6,5},{7,6},{8,7},{9,8},{10,9... | collective-permute-start | bytes 442376 | tf_op jit(solution)/shard_map/ppermute | solution.py:37
  23.8 15.3 %collective-permute-start.7 = (bf16[192,384]{1,0:T(8,128)(2,1)S(1)}, bf16[192,384]{1,0:T(8,128)(2,1)S(1)}, u32[]{:S(2)}, u32[]{:S(2)}) collective-permute-start(bf16[192,384]{1,0:T(8,128)(2,1)S(1)} %get-tuple-element.156), channel_id=1, source_target_pairs={{0,192},{64,128},{128,64},{192,0},{1,193},{65,129},{129,65},{193,1... | collective-permute-start | bytes 442376 | tf_op jit(solution)/shard_map/ppermute | solution.py:32
  26.9 7.3 %collective-permute-start.6 = (bf16[192,384]{1,0:T(8,128)(2,1)S(1)}, bf16[192,384]{1,0:T(8,128)(2,1)S(1)}, u32[]{:S(2)}, u32[]{:S(2)}) collective-permute-start(bf16[192,384]{1,0:T(8,128)(2,1)S(1)} %get-tuple-element.157), channel_id=1, source_target_pairs={{0,128},{64,192},{128,0},{192,64},{1,129},{65,193},{129,1},{193,65... | collective-permute-start | bytes 442376 | tf_op jit(solution)/shard_map/ppermute | solution.py:32
  26.9 13.1 %collective-permute-start.5 = (bf16[192,384]{1,0:T(8,128)(2,1)S(1)}, bf16[192,384]{1,0:T(8,128)(2,1)S(1)}, u32[]{:S(2)}, u32[]{:S(2)}) collective-permute-start(bf16[192,384]{1,0:T(8,128)(2,1)S(1)} %get-tuple-element.158), channel_id=1, source_target_pairs={{0,64},{64,0},{128,192},{192,128},{1,65},{65,1},{129,193},{193,129... | collective-permute-start | bytes 442376 | tf_op jit(solution)/shard_map/ppermute | solution.py:32
  28.3 18.2 %collective-permute-start.8 = (bf16[160,1536]{1,0:T(8,128)(2,1)S(1)}, bf16[160,1536]{1,0:T(8,128)(2,1)S(1)}, u32[]{:S(2)}, u32[]{:S(2)}) collective-permute-start(bf16[160,1536]{1,0:T(8,128)(2,1)S(1)} %get-tuple-element.160), channel_id=1, source_target_pairs={{0,128},{128,0},{1,129},{129,1},{2,130},{130,2},{3,131},{131,3},{4... | collective-permute-start | bytes 1474568 | tf_op jit(solution)/shard_map/ppermute | solution.py:32
  34.3 16.8 %collective-permute-start.10 = (bf16[24,1536]{1,0:T(8,128)(2,1)S(1)}, bf16[24,1536]{1,0:T(8,128)(2,1)S(1)}, u32[]{:S(2)}, u32[]{:S(2)}) collective-permute-start(bf16[24,1536]{1,0:T(8,128)(2,1)S(1)} %pad_maximum_fusion.19), channel_id=1, source_target_pairs={{0,48},{16,32},{32,16},{48,0},{1,49},{17,33},{33,17},{49,1},{2,50}... | collective-permute-start | bytes 221192 | tf_op jit(solution)/shard_map/ppermute | solution.py:32
  37.3 14.3 %collective-permute-start.11 = (bf16[24,1536]{1,0:T(8,128)(2,1)S(1)}, bf16[24,1536]{1,0:T(8,128)(2,1)S(1)}, u32[]{:S(2)}, u32[]{:S(2)}) collective-permute-start(bf16[24,1536]{1,0:T(8,128)(2,1)S(1)} %pad_maximum_fusion.19), channel_id=1, source_target_pairs={{0,32},{16,48},{32,0},{48,16},{1,33},{17,49},{33,1},{49,17},{2,34}... | collective-permute-start | bytes 221192 | tf_op jit(solution)/shard_map/ppermute | solution.py:32
  39.1 12.5 %collective-permute-start.12 = (bf16[24,1536]{1,0:T(8,128)(2,1)S(1)}, bf16[24,1536]{1,0:T(8,128)(2,1)S(1)}, u32[]{:S(2)}, u32[]{:S(2)}) collective-permute-start(bf16[24,1536]{1,0:T(8,128)(2,1)S(1)} %pad_maximum_fusion.19), channel_id=1, source_target_pairs={{0,16},{16,0},{32,48},{48,32},{1,17},{17,1},{33,49},{49,33},{2,18}... | collective-permute-start | bytes 221192 | tf_op jit(solution)/shard_map/ppermute | solution.py:32
  46.6 7.7 %collective-permute-start.13 = (bf16[2,160,1536]{2,1,0:T(8,128)(2,1)S(1)}, bf16[2,160,1536]{2,1,0:T(8,128)(2,1)S(1)}, u32[]{:S(2)}, u32[]{:S(2)}) collective-permute-start(bf16[2,160,1536]{2,1,0:T(8,128)(2,1)S(1)} %pad_maximum_fusion.1), channel_id=1, source_target_pairs={{0,64},{64,0},{1,65},{65,1},{2,66},{66,2},{3,67},{67,3},{4,68},{68... | collective-permute-start | bytes 2949128 | tf_op jit(solution)/shard_map/ppermute | solution.py:32
  54.5 22.0 %collective-permute-start.17 = (bf16[4,24,1536]{2,1,0:T(8,128)(2,1)S(1)}, bf16[4,24,1536]{2,1,0:T(8,128)(2,1)S(1)}, u32[]{:S(2)}, u32[]{:S(2)}) collective-permute-start(bf16[4,24,1536]{2,1,0:T(8,128)(2,1)S(1)} %pad_maximum_fusion.10), channel_id=1, source_target_pairs={{0,12},{4,8},{8,4},{12,0},{1,13},{5,9},{9,5},{13,1},{2,14},{6,10},... | collective-permute-start | bytes 884744 | tf_op jit(solution)/shard_map/ppermute | solution.py:32
  58.3 18.2 %collective-permute-start.18 = (bf16[4,24,1536]{2,1,0:T(8,128)(2,1)S(1)}, bf16[4,24,1536]{2,1,0:T(8,128)(2,1)S(1)}, u32[]{:S(2)}, u32[]{:S(2)}) collective-permute-start(bf16[4,24,1536]{2,1,0:T(8,128)(2,1)S(1)} %pad_maximum_fusion.10), channel_id=1, source_target_pairs={{0,8},{4,12},{8,0},{12,4},{1,9},{5,13},{9,1},{13,5},{2,10},{6,14},... | collective-permute-start | bytes 884744 | tf_op jit(solution)/shard_map/ppermute | solution.py:32
  58.3 18.2 %collective-permute-start.19 = (bf16[4,24,1536]{2,1,0:T(8,128)(2,1)S(1)}, bf16[4,24,1536]{2,1,0:T(8,128)(2,1)S(1)}, u32[]{:S(2)}, u32[]{:S(2)}) collective-permute-start(bf16[4,24,1536]{2,1,0:T(8,128)(2,1)S(1)} %pad_maximum_fusion.10), channel_id=1, source_target_pairs={{0,4},{4,0},{8,12},{12,8},{1,5},{5,1},{9,13},{13,9},{2,6},{6,2},{1... | collective-permute-start | bytes 884744 | tf_op jit(solution)/shard_map/ppermute | solution.py:32
  63.6 12.8 %collective-permute-start.16 = (f32[3,384]{1,0:T(4,128)S(1)}, f32[3,384]{1,0:T(4,128)S(1)}, u32[]{:S(2)}, u32[]{:S(2)}) collective-permute-start(f32[3,384]{1,0:T(4,128)S(1)} %pad_maximum_fusion.27), channel_id=1, source_target_pairs={{0,32},{16,48},{32,0},{48,16},{1,33},{17,49},{33,1},{49,17},{2,34}... | collective-permute-start | bytes 13832 | tf_op jit(solution)/shard_map/ppermute | solution.py:32
  94.0 23.9 %collective-permute-start.23 = (bf16[113,1536]{1,0:T(8,128)(2,1)S(1)}, bf16[113,1536]{1,0:T(8,128)(2,1)S(1)}, u32[]{:S(2)}, u32[]{:S(2)}) collective-permute-start(bf16[113,1536]{1,0:T(8,128)(2,1)S(1)} %get-tuple-element.209), channel_id=1, source_target_pairs={{0,8},{4,12},{8,0},{12,4},{1,9},{5,13},{9,1},{13,5},{2,10},{6,14},... | collective-permute-start | bytes 1041416 | tf_op jit(solution)/shard_map/ppermute | solution.py:32
  96.5 21.4 %collective-permute-start.22 = (bf16[113,1536]{1,0:T(8,128)(2,1)S(1)}, bf16[113,1536]{1,0:T(8,128)(2,1)S(1)}, u32[]{:S(2)}, u32[]{:S(2)}) collective-permute-start(bf16[113,1536]{1,0:T(8,128)(2,1)S(1)} %get-tuple-element.207), channel_id=1, source_target_pairs={{0,4},{4,0},{8,12},{12,8},{1,5},{5,1},{9,13},{13,9},{2,6},{6,2},{1... | collective-permute-start | bytes 1041416 | tf_op jit(solution)/shard_map/ppermute | solution.py:32
  101.7 16.2 %collective-permute-start.24 = (bf16[113,1536]{1,0:T(8,128)(2,1)S(1)}, bf16[113,1536]{1,0:T(8,128)(2,1)S(1)}, u32[]{:S(2)}, u32[]{:S(2)}) collective-permute-start(bf16[113,1536]{1,0:T(8,128)(2,1)S(1)} %get-tuple-element.208), channel_id=1, source_target_pairs={{0,12},{4,8},{8,4},{12,0},{1,13},{5,9},{9,5},{13,1},{2,14},{6,10},... | collective-permute-start | bytes 1041416 | tf_op jit(solution)/shard_map/ppermute | solution.py:32
  106.4 11.5 %collective-permute-start.27 = (f32[2,31,384]{2,1,0:T(8,128)S(1)}, f32[2,31,384]{2,1,0:T(8,128)S(1)}, u32[]{:S(2)}, u32[]{:S(2)}) collective-permute-start(f32[2,31,384]{2,1,0:T(8,128)S(1)} %fusion.62), channel_id=1, source_target_pairs={{0,16},{16,0},{32,48},{48,32},{1,17},{17,1},{33,49},{49,33},{2,18}... | collective-permute-start | bytes 285704 | tf_op jit(solution)/shard_map/ppermute | solution.py:32
  108.9 10.9 %collective-permute-start.28 = (bf16[2,128,1536]{2,1,0:T(8,128)(2,1)S(1)}, bf16[2,128,1536]{2,1,0:T(8,128)(2,1)S(1)}, u32[]{:S(2)}, u32[]{:S(2)}) collective-permute-start(bf16[2,128,1536]{2,1,0:T(8,128)(2,1)S(1)} %pad_maximum_fusion.2), channel_id=1, source_target_pairs={{0,64},{64,0},{1,65},{65,1},{2,66},{66,2},{3,67},{67,3},{4,68},{68... | collective-permute-start | bytes 2359304 | tf_op jit(solution)/shard_map/ppermute | solution.py:32
  120.1 9.9 %collective-permute-start.29 = (bf16[128,1536]{1,0:T(8,128)(2,1)S(1)}, bf16[128,1536]{1,0:T(8,128)(2,1)S(1)}, u32[]{:S(2)}, u32[]{:S(2)}) collective-permute-start(bf16[128,1536]{1,0:T(8,128)(2,1)S(1)} %fusion.3), channel_id=1, source_target_pairs={{0,128},{128,0},{1,129},{129,1},{2,130},{130,2},{3,131},{131,3},{4... | collective-permute-start | bytes 1179656 | tf_op jit(solution)/shard_map/ppermute | solution.py:32
  130.2 13.3 %collective-permute-start.30 = (bf16[41,1536]{1,0:T(8,128)(2,1)S(1)}, bf16[41,1536]{1,0:T(8,128)(2,1)S(1)}, u32[]{:S(2)}, u32[]{:S(2)}) collective-permute-start(bf16[41,1536]{1,0:T(8,128)(2,1)S(1)} %get-tuple-element.204), channel_id=1, source_target_pairs={{0,16},{16,0},{32,48},{48,32},{1,17},{17,1},{33,49},{49,33},{2,18}... | collective-permute-start | bytes 377864 | tf_op jit(solution)/shard_map/ppermute | solution.py:32
  130.3 7.0 %collective-permute-start.33 = (f32[2,31,384]{2,1,0:T(8,128)S(1)}, f32[2,31,384]{2,1,0:T(8,128)S(1)}, u32[]{:S(2)}, u32[]{:S(2)}) collective-permute-start(f32[2,31,384]{2,1,0:T(8,128)S(1)} %add.418), channel_id=1, source_target_pairs={{0,4},{4,0},{8,12},{12,8},{1,5},{5,1},{9,13},{13,9},{2,6},{6,2},{1... | collective-permute-start | bytes 285704 | tf_op jit(solution)/shard_map/ppermute | solution.py:32
  131.6 12.4 %collective-permute-start.32 = (bf16[41,1536]{1,0:T(8,128)(2,1)S(1)}, bf16[41,1536]{1,0:T(8,128)(2,1)S(1)}, u32[]{:S(2)}, u32[]{:S(2)}) collective-permute-start(bf16[41,1536]{1,0:T(8,128)(2,1)S(1)} %get-tuple-element.206), channel_id=1, source_target_pairs={{0,48},{16,32},{32,16},{48,0},{1,49},{17,33},{33,17},{49,1},{2,50}... | collective-permute-start | bytes 377864 | tf_op jit(solution)/shard_map/ppermute | solution.py:32
  132.6 11.4 %collective-permute-start.31 = (bf16[41,1536]{1,0:T(8,128)(2,1)S(1)}, bf16[41,1536]{1,0:T(8,128)(2,1)S(1)}, u32[]{:S(2)}, u32[]{:S(2)}) collective-permute-start(bf16[41,1536]{1,0:T(8,128)(2,1)S(1)} %get-tuple-element.205), channel_id=1, source_target_pairs={{0,32},{16,48},{32,0},{48,16},{1,33},{17,49},{33,1},{49,17},{2,34}... | collective-permute-start | bytes 377864 | tf_op jit(solution)/shard_map/ppermute | solution.py:32
  144.4 9.0 %collective-permute-start.35 = (bf16[23,1536]{1,0:T(8,128)(2,1)S(1)}, bf16[23,1536]{1,0:T(8,128)(2,1)S(1)}, u32[]{:S(2)}, u32[]{:S(2)}) collective-permute-start(bf16[23,1536]{1,0:T(8,128)(2,1)S(1)} %get-tuple-element.199), channel_id=1, source_target_pairs={{0,1},{1,0},{2,3},{3,2},{4,5},{5,4},{6,7},{7,6},{8,9},{9,8},{10,11... | collective-permute-start | bytes 211976 | tf_op jit(solution)/shard_map/ppermute | solution.py:32
  145.6 7.8 %collective-permute-start.36 = (bf16[23,1536]{1,0:T(8,128)(2,1)S(1)}, bf16[23,1536]{1,0:T(8,128)(2,1)S(1)}, u32[]{:S(2)}, u32[]{:S(2)}) collective-permute-start(bf16[23,1536]{1,0:T(8,128)(2,1)S(1)} %get-tuple-element.198), channel_id=1, source_target_pairs={{0,2},{1,3},{2,0},{3,1},{4,6},{5,7},{6,4},{7,5},{8,10},{9,11},{10,... | collective-permute-start | bytes 211976 | tf_op jit(solution)/shard_map/ppermute | solution.py:32
  148.4 14.1 %collective-permute-start.41 = (f32[2,31,384]{2,1,0:T(8,128)S(1)}, f32[2,31,384]{2,1,0:T(8,128)S(1)}, u32[]{:S(2)}, u32[]{:S(2)}) collective-permute-start(f32[2,31,384]{2,1,0:T(8,128)S(1)} %add.441), channel_id=1, source_target_pairs={{0,32},{16,48},{32,0},{48,16},{1,33},{17,49},{33,1},{49,17},{2,34}... | collective-permute-start | bytes 285704 | tf_op jit(solution)/shard_map/ppermute | solution.py:32
  156.6 14.5 %collective-permute-start.38 = (bf16[128,384]{1,0:T(8,128)(2,1)S(1)}, bf16[128,384]{1,0:T(8,128)(2,1)S(1)}, u32[]{:S(2)}, u32[]{:S(2)}) collective-permute-start(bf16[128,384]{1,0:T(8,128)(2,1)S(1)} %get-tuple-element.163), channel_id=1, source_target_pairs={{0,192},{64,128},{128,64},{192,0},{1,193},{65,129},{129,65},{193,1... | collective-permute-start | bytes 294920 | tf_op jit(solution)/shard_map/ppermute | solution.py:32
  162.5 8.6 %collective-permute-start.39 = (bf16[128,384]{1,0:T(8,128)(2,1)S(1)}, bf16[128,384]{1,0:T(8,128)(2,1)S(1)}, u32[]{:S(2)}, u32[]{:S(2)}) collective-permute-start(bf16[128,384]{1,0:T(8,128)(2,1)S(1)} %get-tuple-element.162), channel_id=1, source_target_pairs={{0,128},{64,192},{128,0},{192,64},{1,129},{65,193},{129,1},{193,65... | collective-permute-start | bytes 294920 | tf_op jit(solution)/shard_map/ppermute | solution.py:32
  (30 other events, 239.4 us)
where the time goes:
time: 172 us
  starting transfers between devices  86.8 us (50%)
  waiting for transfers between devices  47.5 us (28%)
  Pallas kernels  14.9 us (9%)
  other arithmetic  7.6 us (4%)
  local copies, waits for them, and re-layouts  7.56 us (4%)
  matrix products  5.32 us (3%)
  between operations  2.28 us (1%)
    ppermute x43, starting transfers between devices, swap(): return lax.ppermute(value, axis, [(i, i ^ mask) for i in range(size(axis))])  76 us
    ppermute x43, waiting for transfers between devices, swap(): return lax.ppermute(value, axis, [(i, i ^ mask) for i in range(size(axis))])  42 us
    pallas_call x4, Pallas kernels, by_lanes(): pl.pallas_call(kernel, out_shape=shapes, grid_spec=pltpu.PrefetchScalarGr...  14.9 us
    ppermute x2, starting transfers between devices, shift(): lax.ppermute(value, axis, [(i, (i + step) % count) for i in range(count)])  10.8 us
    ppermute x2, waiting for transfers between devices, shift(): lax.ppermute(value, axis, [(i, (i + step) % count) for i in range(count)])  5.47 us
  transfers between devices with their start and end apart: 45, of which 18 were waited for; matrix products, arithmetic and copies ran while one was open for 5% of the time, Pallas kernels for 7%

commit v1 on v0

--- a/solution.py
+++ b/solution.py
@@ -51,6 +51,13 @@
 
 barrier = lax.optimization_barrier
 STAGES = (("x", 1), ("x", 2), ("zh", 1), ("zh", 2), ("y", 1), ("y", 2))
+
+
+def side_by_side(table, axis):
+    other = swap(table, axis, 1)
+    second = lax.axis_index(axis) == 1
+    parts = [jnp.where(second, other, table), jnp.where(second, table, other)]
+    return jnp.concatenate(parts, axis=1)
 
 
 def halves(value):
@@ -318,10 +325,10 @@
         [((4, frames, own), bf16), ((4, span, own), f32), ((KERNEL + 3, own), f32)],
         meta=meta,
     )
-    stats, tap_in, tap_off, sums = barrier((stats, tap_in, tap_off, sums))
     channel_mean = stats[1:2]
     inv_std = lax.rsqrt(stats[2:3] / count + norm_eps)
-    tap_pair = jnp.stack([tap_in, inv_std * (tap_off + (mean - channel_mean) * tap_in)])
+    tap_off = inv_std * (tap_off + (mean - channel_mean) * tap_in)
+    sums = jnp.concatenate([sums, tap_in, tap_off])
 
     flat = hidden.reshape(4 * frames, own)
     weight_grad = lax.dot_general(
@@ -336,16 +343,9 @@
     other = swap(jnp.stack([product[1], product[3]]).astype(bf16), "core", 1).astype(f32)
     kept, far = product[0] + other[0], product[2] + other[1]
     product = kept + swap(far.astype(bf16), "zl", 1).astype(f32)
-    for axis, mask in STAGES[:3]:
-        tap_pair = tap_pair + swap(tap_pair, axis, mask)
-    weight_grad, sums, tap_pair, product = barrier((weight_grad, sums, tap_pair, product))
+    weight_grad, sums, product = barrier((weight_grad, sums, product))
     weight_grad, sums = scatter_stage(weight_grad, sums, "zh", 0)
-    for axis, mask in STAGES[4:]:
-        tap_pair = tap_pair + swap(tap_pair, axis, mask)
-    weight_grad, sums, tap_pair = barrier((weight_grad, sums, tap_pair))
     weight_grad, sums = scatter_stage(weight_grad.reshape(4, own // 64, width), sums, "x", 0)
-    for axis, mask in STAGES[3:4]:
-        tap_pair = tap_pair + swap(tap_pair, axis, mask)
     stream_valid = (seq * frames + jnp.arange(frames, dtype=jnp.int32) < limit[0])[:, None]
     module_out = jnp.where(stream_valid, product, 0.0).astype(bf16)
 
@@ -358,13 +358,15 @@
     )
     _, sums = barrier((flipped, sums))
     gain_grad, bias_grad = sums[KERNEL : KERNEL + 1], sums[KERNEL + 1 : KERNEL + 2]
+    tap_in, tap_off = sums[KERNEL + 3 : 2 * KERNEL + 3], sums[2 * KERNEL + 3 :]
     tap_sums = (inv_std * gain_own) * (
-        sums[:KERNEL] - bias_grad / count * tap_pair[0] - gain_grad / count * tap_pair[1]
+        sums[:KERNEL] - bias_grad / count * tap_in - gain_grad / count * tap_off
     )
     table = jnp.concatenate([tap_sums, sums[KERNEL : KERNEL + 2]], axis=0)
-    parts = [flipped[0]] + [swap(flipped[m], DP, m) for m in (1, 2, 3)]
-    input_grad = jnp.concatenate(in_order(dp, parts), axis=1)
-    table = jnp.concatenate(in_order(dp, exchange(table, DP)), axis=1)
+    near = swap(jnp.stack([flipped[1], flipped[3]]), "core", 1)
+    far = swap(jnp.stack([flipped[2], near[1]]), "zl", 1)
+    input_grad = jnp.concatenate(in_order(dp, [flipped[0], near[0], far[0], far[1]]), axis=1)
+    table = side_by_side(side_by_side(table, "core"), "zl")
 
     new_one = beta_one * moment_one + (1.0 - beta_one) * weight_grad
     new_two = beta_two * moment_two + (1.0 - beta_two) * weight_grad * weight_grad

time: 172 us -> 182 us (1.058); the launches traced: 172 us -> 179 us
  waiting for transfers between devices: 47.5 us -> 73.7 us
  starting transfers between devices: 86.8 us -> 67.9 us
    ppermute x43 -> x35, waiting for transfers between devices: 42 us -> 68.2 us  [swap(): return lax.ppermute(value, axis, [(i, i ^ mask) for i in range(size(axis))])]
    ppermute x43 -> x35, starting transfers between devices: 76 us -> 57.1 us  [swap(): return lax.ppermute(value, axis, [(i, i ^ mask) for i in range(size(axis))])]
  transfers between devices with their start and end apart: 45 -> 37, of which waited for: 18 -> 21; matrix products, arithmetic and copies ran while one was open for 5% -> 5% of each run, Pallas kernels for 7% -> 5%
where the time goes in v1:
time: 182 us; the launch traced here: 179 us
  waiting for transfers between devices  73.7 us (40%)
  starting transfers between devices  67.9 us (37%)
  Pallas kernels  14.9 us (8%)
  other arithmetic  8.45 us (5%)
  local copies, waits for them, and re-layouts  6.88 us (4%)
  matrix products  5.31 us (3%)
  between operations  2.24 us (1%)
    ppermute x35, waiting for transfers between devices, swap(): return lax.ppermute(value, axis, [(i, i ^ mask) for i in range(size(axis))])  68.2 us
    ppermute x35, starting transfers between devices, swap(): return lax.ppermute(value, axis, [(i, i ^ mask) for i in range(size(axis))])  57.1 us
    pallas_call x4, Pallas kernels, by_lanes(): pl.pallas_call(kernel, out_shape=shapes, grid_spec=pltpu.PrefetchScalarGr...  14.9 us
    ppermute x2, starting transfers between devices, shift(): lax.ppermute(value, axis, [(i, (i + step) % count) for i in range(count)])  10.8 us
    ppermute x2, waiting for transfers between devices, shift(): lax.ppermute(value, axis, [(i, (i + step) % count) for i in range(count)])  5.46 us
  transfers between devices with their start and end apart: 37, of which 21 were waited for; matrix products, arithmetic and copies ran while one was open for 5% of the time, Pallas kernels for 5%

profile of v1, /device:TPU:1, one launch (start us, length us, event | category | flops | bytes accessed | tf_op | source)
XLA Modules:
  0.0 179.3 jit_solution(13887261029938895783)
XLA Ops:
  2.6 2.1 %collective-permute-start.2 = (bf16[6,1536]{1,0:T(8,128)(2,1)}, bf16[6,1536]{1,0:T(8,128)(2,1)S(1)}, u32[]{:S(2)}, u32[]{:S(2)}) collective-permute-start(bf16[6,1536]{1,0:T(8,128)(2,1)} %param.15), channel_id=1, source_target_pairs={{0,1},{1,0},{2,3},{3,2},{4,5},{5,4},{6,7},{7,6},{8,9},{9,8},{10,11... | collective-permute-start | bytes 55304 | tf_op jit(solution)/shard_map/ppermute | solution.py:32
  4.7 2.5 %collective-permute-start.3 = (bf16[6,1536]{1,0:T(8,128)(2,1)}, bf16[6,1536]{1,0:T(8,128)(2,1)S(1)}, u32[]{:S(2)}, u32[]{:S(2)}) collective-permute-start(bf16[6,1536]{1,0:T(8,128)(2,1)} %param.15), channel_id=1, source_target_pairs={{0,2},{1,3},{2,0},{3,1},{4,6},{5,7},{6,4},{7,5},{8,10},{9,11},{10,... | collective-permute-start | bytes 55304 | tf_op jit(solution)/shard_map/ppermute | solution.py:32
  7.3 10.7 %collective-permute-start.1 = (bf16[48,1536]{1,0:T(8,128)(2,1)S(1)}, bf16[48,1536]{1,0:T(8,128)(2,1)S(1)}, u32[]{:S(2)}, u32[]{:S(2)}) collective-permute-start(bf16[48,1536]{1,0:T(8,128)(2,1)S(1)} %get-tuple-element.53), channel_id=1, source_target_pairs={{0,63},{1,0},{2,1},{3,2},{4,3},{5,4},{6,5},{7,6},{8,7},{9,8},{10,9... | collective-permute-start | bytes 442376 | tf_op jit(solution)/shard_map/ppermute | solution.py:37
  18.1 3.6 %collective-permute-done = bf16[48,1536]{1,0:T(8,128)(2,1)S(1)} collective-permute-done((bf16[48,1536]{1,0:T(8,128)(2,1)S(1)}, bf16[48,1536]{1,0:T(8,128)(2,1)S(1)}, u32[]{:S(2)}, u32[]{:S(2)}) %collective-permute-start) | collective-permute-done | bytes 147488 | tf_op jit(solution)/shard_map/ppermute | solution.py:37
  23.8 3.1 %collective-permute-start.7 = (bf16[192,384]{1,0:T(8,128)(2,1)S(1)}, bf16[192,384]{1,0:T(8,128)(2,1)S(1)}, u32[]{:S(2)}, u32[]{:S(2)}) collective-permute-start(bf16[192,384]{1,0:T(8,128)(2,1)S(1)} %get-tuple-element.143), channel_id=1, source_target_pairs={{0,192},{64,128},{128,64},{192,0},{1,193},{65,129},{129,65},{193,1... | collective-permute-start | bytes 442376 | tf_op jit(solution)/shard_map/ppermute | solution.py:32
  30.2 4.0 %collective-permute-done.6 = bf16[192,384]{1,0:T(8,128)(2,1)S(1)} collective-permute-done((bf16[192,384]{1,0:T(8,128)(2,1)S(1)}, bf16[192,384]{1,0:T(8,128)(2,1)S(1)}, u32[]{:S(2)}, u32[]{:S(2)}) %collective-permute-start.6) | collective-permute-done | bytes 147488 | tf_op jit(solution)/shard_map/ppermute | solution.py:32
  34.3 3.0 %collective-permute-start.10 = (bf16[24,1536]{1,0:T(8,128)(2,1)S(1)}, bf16[24,1536]{1,0:T(8,128)(2,1)S(1)}, u32[]{:S(2)}, u32[]{:S(2)}) collective-permute-start(bf16[24,1536]{1,0:T(8,128)(2,1)S(1)} %pad_maximum_fusion.25), channel_id=1, source_target_pairs={{0,48},{16,32},{32,16},{48,0},{1,49},{17,33},{33,17},{49,1},{2,50}... | collective-permute-start | bytes 221192 | tf_op jit(solution)/shard_map/ppermute | solution.py:32
  40.1 3.5 %shard_map.161 = (f32[4,192,384]{2,1,0:T(8,128)S(1)}, f32[4,160,384]{2,1,0:T(8,128)S(1)}, f32[3,384]{1,0:T(4,128)S(1)}) custom-call(s32[6]{0:T(128)S(1)} %pad_add_fusion.meta_ref, bf16[4,192,384]{2,1,0:T(8,128)(2,1)S(1)} %pad_maximum_fusion.4.slab_ref, f32[31,384]{1,0:T(8,128)S(1)} %constant_dynamic-slice_fusion.taps_ref), custom_call_target="tpu_custom_call" | custom-call | tf_op jit(solution)/shard_map/pallas_call | solution.py:228
  43.6 2.9 %collective-permute-done.8 = bf16[160,1536]{1,0:T(8,128)(2,1)S(1)} collective-permute-done((bf16[160,1536]{1,0:T(8,128)(2,1)S(1)}, bf16[160,1536]{1,0:T(8,128)(2,1)S(1)}, u32[]{:S(2)}, u32[]{:S(2)}) %collective-permute-start.8) | collective-permute-done | bytes 491552 | tf_op jit(solution)/shard_map/ppermute | solution.py:32
  48.6 2.5 %collective-permute-done.10 = bf16[24,1536]{1,0:T(8,128)(2,1)S(1)} collective-permute-done((bf16[24,1536]{1,0:T(8,128)(2,1)S(1)}, bf16[24,1536]{1,0:T(8,128)(2,1)S(1)}, u32[]{:S(2)}, u32[]{:S(2)}) %collective-permute-start.10) | collective-permute-done | bytes 73760 | tf_op jit(solution)/shard_map/ppermute | solution.py:32
  51.9 2.4 %collective-permute-done.9 = f32[3,384]{1,0:T(4,128)S(1)} collective-permute-done((f32[3,384]{1,0:T(4,128)S(1)}, f32[3,384]{1,0:T(4,128)S(1)}, u32[]{:S(2)}, u32[]{:S(2)}) %collective-permute-start.9) | collective-permute-done | bytes 4640 | tf_op jit(solution)/shard_map/ppermute | solution.py:32
  54.5 3.8 %collective-permute-start.17 = (bf16[4,24,1536]{2,1,0:T(8,128)(2,1)S(1)}, bf16[4,24,1536]{2,1,0:T(8,128)(2,1)S(1)}, u32[]{:S(2)}, u32[]{:S(2)}) collective-permute-start(bf16[4,24,1536]{2,1,0:T(8,128)(2,1)S(1)} %pad_maximum_fusion.10), channel_id=1, source_target_pairs={{0,12},{4,8},{8,4},{12,0},{1,13},{5,9},{9,5},{13,1},{2,14},{6,10},... | collective-permute-start | bytes 884744 | tf_op jit(solution)/shard_map/ppermute | solution.py:32
  59.0 3.6 %collective-permute-start.15 = (f32[3,384]{1,0:T(4,128)S(1)}, f32[3,384]{1,0:T(4,128)S(1)}, u32[]{:S(2)}, u32[]{:S(2)}) collective-permute-start(f32[3,384]{1,0:T(4,128)S(1)} %pad_maximum_fusion.29), channel_id=1, source_target_pairs={{0,16},{16,0},{32,48},{48,32},{1,17},{17,1},{33,49},{49,33},{2,18}... | collective-permute-start | bytes 13832 | tf_op jit(solution)/shard_map/ppermute | solution.py:32
  63.6 6.3 %collective-permute-start.16 = (f32[3,384]{1,0:T(4,128)S(1)}, f32[3,384]{1,0:T(4,128)S(1)}, u32[]{:S(2)}, u32[]{:S(2)}) collective-permute-start(f32[3,384]{1,0:T(4,128)S(1)} %pad_maximum_fusion.30), channel_id=1, source_target_pairs={{0,32},{16,48},{32,0},{48,16},{1,33},{17,49},{33,1},{49,17},{2,34}... | collective-permute-start | bytes 13832 | tf_op jit(solution)/shard_map/ppermute | solution.py:32
  71.5 4.9 %shard_map.162 = (f32[31,384]{1,0:T(8,128)S(1)}, f32[31,384]{1,0:T(8,128)S(1)}) custom-call(s32[6]{0:T(128)S(1)} %pad_add_fusion.meta_ref, f32[4,192,384]{2,1,0:T(8,128)S(1)} %get-tuple-element.79.masked_ref, f32[4,160,384]{2,1,0:T(8,128)S(1)} %get-tuple-element.66.conv_ref, f32[1,384]{1,0:T(1,128)S(1)} %slice.500.mean_ref), custom_call_target="tpu_custom_call" | custom-call | tf_op jit(solution)/shard_map/pallas_call | solution.py:228
  76.9 2.1 %fusion.57.back_ref = f32[4,160,384]{2,1,0:T(8,128)} fusion(bf16[4,160,1536]{2,1,0:T(8,128)(2,1)S(1)} %maximum_select_fusion, bf16[384,1536,1]{1,0,2:T(8,128)(2,1)S(1)} %bitcast.121), kind=kOutput, calls=%fused_computation.243 | convolution fusion | flops 754974720 | bytes 4128768 | tf_op jit(solution)/shard_map/dot_general | solution.py:302
  81.6 2.5 %collective-permute-start.21 = (f32[3,384]{1,0:T(4,128)S(1)}, f32[3,384]{1,0:T(4,128)S(1)}, u32[]{:S(2)}, u32[]{:S(2)}) collective-permute-start(f32[3,384]{1,0:T(4,128)S(1)} %pad_maximum_fusion.32), channel_id=1, source_target_pairs={{0,8},{4,12},{8,0},{12,4},{1,9},{5,13},{9,1},{13,5},{2,10},{6,14},... | collective-permute-start | bytes 13832 | tf_op jit(solution)/shard_map/ppermute | solution.py:32
  86.9 3.5 %shard_map.163 = (bf16[4,128,384]{2,1,0:T(8,128)(2,1)S(1)}, f32[4,160,384]{2,1,0:T(8,128)S(1)}, f32[34,384]{1,0:T(8,128)S(1)}) custom-call(s32[6]{0:T(128)S(1)} %pad_add_fusion.meta_ref, f32[4,160,384]{2,1,0:T(8,128)S(1)} %get-tuple-element.66.conv_ref, f32[4,160,384]{2,1,0:T(8,128)S(1)} %copy-done.1, f32[4,192,384]{2,1,0:T(8,128)S(1)} %get-tuple-element.79.masked_ref, ...), custom_call_target="tpu_custom_call" | custom-call | tf_op jit(solution)/shard_map/pallas_call | solution.py:228
  91.7 2.2 %fusion = f32[4,4,24,1536]{3,2,1,0:T(8,128)S(1)} fusion(bf16[4,4,24,512]{3,2,1,0:T(8,128)(2,1)S(1)} %bitcast.126, bf16[512,1536]{1,0:T(8,128)(2,1)} %bitcast.120), kind=kOutput, calls=%fused_computation.1 | convolution fusion | flops 603979776 | bytes 4325376 | tf_op jit(solution)/shard_map/dot_general | solution.py:334
  94.1 2.7 %collective-permute-start.24 = (bf16[144,1536]{1,0:T(8,128)(2,1)S(1)}, bf16[144,1536]{1,0:T(8,128)(2,1)S(1)}, u32[]{:S(2)}, u32[]{:S(2)}) collective-permute-start(bf16[144,1536]{1,0:T(8,128)(2,1)S(1)} %get-tuple-element.199), channel_id=1, source_target_pairs={{0,12},{4,8},{8,4},{12,0},{1,13},{5,9},{9,5},{13,1},{2,14},{6,10},... | collective-permute-start | bytes 1327112 | tf_op jit(solution)/shard_map/ppermute | solution.py:32
  98.7 6.2 %collective-permute-start.25 = (bf16[2,128,1536]{2,1,0:T(8,128)(2,1)S(1)}, bf16[2,128,1536]{2,1,0:T(8,128)(2,1)S(1)}, u32[]{:S(2)}, u32[]{:S(2)}) collective-permute-start(bf16[2,128,1536]{2,1,0:T(8,128)(2,1)S(1)} %pad_maximum_fusion.2), channel_id=1, source_target_pairs={{0,64},{64,0},{1,65},{65,1},{2,66},{66,2},{3,67},{67,3},{4,68},{68... | collective-permute-start | bytes 2359304 | tf_op jit(solution)/shard_map/ppermute | solution.py:32
  104.9 6.9 %collective-permute-done.22 = bf16[144,1536]{1,0:T(8,128)(2,1)S(1)} collective-permute-done((bf16[144,1536]{1,0:T(8,128)(2,1)S(1)}, bf16[144,1536]{1,0:T(8,128)(2,1)S(1)}, u32[]{:S(2)}, u32[]{:S(2)}) %collective-permute-start.22) | collective-permute-done | bytes 442400 | tf_op jit(solution)/shard_map/ppermute | solution.py:32
  111.8 3.2 %collective-permute-done.24 = bf16[144,1536]{1,0:T(8,128)(2,1)S(1)} collective-permute-done((bf16[144,1536]{1,0:T(8,128)(2,1)S(1)}, bf16[144,1536]{1,0:T(8,128)(2,1)S(1)}, u32[]{:S(2)}, u32[]{:S(2)}) %collective-permute-start.24) | collective-permute-done | bytes 442400 | tf_op jit(solution)/shard_map/ppermute | solution.py:32
  116.4 5.8 %collective-permute-done.26 = bf16[128,1536]{1,0:T(8,128)(2,1)S(1)} collective-permute-done((bf16[128,1536]{1,0:T(8,128)(2,1)S(1)}, bf16[128,1536]{1,0:T(8,128)(2,1)S(1)}, u32[]{:S(2)}, u32[]{:S(2)}) %collective-permute-start.26) | collective-permute-done | bytes 393248 | tf_op jit(solution)/shard_map/ppermute | solution.py:32
  122.5 4.5 %collective-permute-start.29 = (bf16[72,1536]{1,0:T(8,128)(2,1)S(1)}, bf16[72,1536]{1,0:T(8,128)(2,1)S(1)}, u32[]{:S(2)}, u32[]{:S(2)}) collective-permute-start(bf16[72,1536]{1,0:T(8,128)(2,1)S(1)} %get-tuple-element.193), channel_id=1, source_target_pairs={{0,48},{16,32},{32,16},{48,0},{1,49},{17,33},{33,17},{49,1},{2,50}... | collective-permute-start | bytes 663560 | tf_op jit(solution)/shard_map/ppermute | solution.py:32
  130.1 16.2 %collective-permute-done.29 = bf16[72,1536]{1,0:T(8,128)(2,1)S(1)} collective-permute-done((bf16[72,1536]{1,0:T(8,128)(2,1)S(1)}, bf16[72,1536]{1,0:T(8,128)(2,1)S(1)}, u32[]{:S(2)}, u32[]{:S(2)}) %collective-permute-start.29) | collective-permute-done | bytes 221216 | tf_op jit(solution)/shard_map/ppermute | solution.py:32
  146.4 3.0 %collective-permute-done.27 = bf16[72,1536]{1,0:T(8,128)(2,1)S(1)} collective-permute-done((bf16[72,1536]{1,0:T(8,128)(2,1)S(1)}, bf16[72,1536]{1,0:T(8,128)(2,1)S(1)}, u32[]{:S(2)}, u32[]{:S(2)}) %collective-permute-start.27) | collective-permute-done | bytes 221216 | tf_op jit(solution)/shard_map/ppermute | solution.py:32
  155.3 4.2 %collective-permute-done.31 = bf16[54,1536]{1,0:T(8,128)(2,1)S(1)} collective-permute-done((bf16[54,1536]{1,0:T(8,128)(2,1)S(1)}, bf16[54,1536]{1,0:T(8,128)(2,1)S(1)}, u32[]{:S(2)}, u32[]{:S(2)}) %collective-permute-start.31) | collective-permute-done | bytes 165920 | tf_op jit(solution)/shard_map/ppermute | solution.py:32
  159.5 2.7 %collective-permute-done.32 = bf16[54,1536]{1,0:T(8,128)(2,1)S(1)} collective-permute-done((bf16[54,1536]{1,0:T(8,128)(2,1)S(1)}, bf16[54,1536]{1,0:T(8,128)(2,1)S(1)}, u32[]{:S(2)}, u32[]{:S(2)}) %collective-permute-start.32) | collective-permute-done | bytes 165920 | tf_op jit(solution)/shard_map/ppermute | solution.py:32
  162.4 3.0 %shard_map.164 = bf16[4,128,384]{2,1,0:T(8,128)(2,1)S(1)} custom-call(s32[6]{0:T(128)S(1)} %pad_add_fusion.meta_ref, f32[4,160,384]{2,1,0:T(8,128)S(1)} %get-tuple-element.66.conv_ref, f32[4,160,384]{2,1,0:T(8,128)S(1)} %copy-done.3, f32[3,384]{1,0:T(4,128)S(1)} %pad_maximum_fusion.33.stats_ref, f32[2,384]{1,0:T(2,128)S(1)} %fusion.30.affine_ref, ...), custom_call_target="tpu_custom_call" | custom-call | tf_op jit(solution)/shard_map/pallas_call | solution.py:228
  168.6 3.8 %collective-permute-done.36 = f32[33,768]{1,0:T(8,128)S(1)} collective-permute-done((f32[33,768]{1,0:T(8,128)S(1)}, f32[33,768]{1,0:T(8,128)S(1)}, u32[]{:S(2)}, u32[]{:S(2)}) %collective-permute-start.36) | collective-permute-done | bytes 101408 | tf_op jit(solution)/shard_map/ppermute | solution.py:32
  174.3 4.2 %collective-permute-done.34 = bf16[2,128,384]{2,1,0:T(8,128)(2,1)S(1)} collective-permute-done((bf16[2,128,384]{2,1,0:T(8,128)(2,1)S(1)}, bf16[2,128,384]{2,1,0:T(8,128)(2,1)S(1)}, u32[]{:S(2)}, u32[]{:S(2)}) %collective-permute-start.34) | collective-permute-done | bytes 196640 | tf_op jit(solution)/shard_map/ppermute | solution.py:32
  (190 shorter events, 41.5 us)
Async XLA Ops:
  2.6 15.5 %collective-permute-start.2 = (bf16[6,1536]{1,0:T(8,128)(2,1)}, bf16[6,1536]{1,0:T(8,128)(2,1)S(1)}, u32[]{:S(2)}, u32[]{:S(2)}) collective-permute-start(bf16[6,1536]{1,0:T(8,128)(2,1)} %param.15), channel_id=1, source_target_pairs={{0,1},{1,0},{2,3},{3,2},{4,5},{5,4},{6,7},{7,6},{8,9},{9,8},{10,11... | collective-permute-start | bytes 55304 | tf_op jit(solution)/shard_map/ppermute | solution.py:32
  4.7 13.4 %collective-permute-start.3 = (bf16[6,1536]{1,0:T(8,128)(2,1)}, bf16[6,1536]{1,0:T(8,128)(2,1)S(1)}, u32[]{:S(2)}, u32[]{:S(2)}) collective-permute-start(bf16[6,1536]{1,0:T(8,128)(2,1)} %param.15), channel_id=1, source_target_pairs={{0,2},{1,3},{2,0},{3,1},{4,6},{5,7},{6,4},{7,5},{8,10},{9,11},{10,... | collective-permute-start | bytes 55304 | tf_op jit(solution)/shard_map/ppermute | solution.py:32
  7.1 11.0 %collective-permute-start.4 = (bf16[6,1536]{1,0:T(8,128)(2,1)}, bf16[6,1536]{1,0:T(8,128)(2,1)S(1)}, u32[]{:S(2)}, u32[]{:S(2)}) collective-permute-start(bf16[6,1536]{1,0:T(8,128)(2,1)} %param.15), channel_id=1, source_target_pairs={{0,3},{1,2},{2,1},{3,0},{4,7},{5,6},{6,5},{7,4},{8,11},{9,10},{10,... | collective-permute-start | bytes 55304 | tf_op jit(solution)/shard_map/ppermute | solution.py:32
  7.2 14.5 %collective-permute-start = (bf16[48,1536]{1,0:T(8,128)(2,1)S(1)}, bf16[48,1536]{1,0:T(8,128)(2,1)S(1)}, u32[]{:S(2)}, u32[]{:S(2)}) collective-permute-start(bf16[48,1536]{1,0:T(8,128)(2,1)S(1)} %get-tuple-element.52), channel_id=1, source_target_pairs={{0,1},{1,2},{2,3},{3,4},{4,5},{5,6},{6,7},{7,8},{8,9},{9,10},{10,1... | collective-permute-start | bytes 442376 | tf_op jit(solution)/shard_map/ppermute | solution.py:37
  7.3 16.2 %collective-permute-start.1 = (bf16[48,1536]{1,0:T(8,128)(2,1)S(1)}, bf16[48,1536]{1,0:T(8,128)(2,1)S(1)}, u32[]{:S(2)}, u32[]{:S(2)}) collective-permute-start(bf16[48,1536]{1,0:T(8,128)(2,1)S(1)} %get-tuple-element.53), channel_id=1, source_target_pairs={{0,63},{1,0},{2,1},{3,2},{4,3},{5,4},{6,5},{7,6},{8,7},{9,8},{10,9... | collective-permute-start | bytes 442376 | tf_op jit(solution)/shard_map/ppermute | solution.py:37
  23.8 15.3 %collective-permute-start.7 = (bf16[192,384]{1,0:T(8,128)(2,1)S(1)}, bf16[192,384]{1,0:T(8,128)(2,1)S(1)}, u32[]{:S(2)}, u32[]{:S(2)}) collective-permute-start(bf16[192,384]{1,0:T(8,128)(2,1)S(1)} %get-tuple-element.143), channel_id=1, source_target_pairs={{0,192},{64,128},{128,64},{192,0},{1,193},{65,129},{129,65},{193,1... | collective-permute-start | bytes 442376 | tf_op jit(solution)/shard_map/ppermute | solution.py:32
  26.9 7.3 %collective-permute-start.6 = (bf16[192,384]{1,0:T(8,128)(2,1)S(1)}, bf16[192,384]{1,0:T(8,128)(2,1)S(1)}, u32[]{:S(2)}, u32[]{:S(2)}) collective-permute-start(bf16[192,384]{1,0:T(8,128)(2,1)S(1)} %get-tuple-element.144), channel_id=1, source_target_pairs={{0,128},{64,192},{128,0},{192,64},{1,129},{65,193},{129,1},{193,65... | collective-permute-start | bytes 442376 | tf_op jit(solution)/shard_map/ppermute | solution.py:32
  26.9 13.1 %collective-permute-start.5 = (bf16[192,384]{1,0:T(8,128)(2,1)S(1)}, bf16[192,384]{1,0:T(8,128)(2,1)S(1)}, u32[]{:S(2)}, u32[]{:S(2)}) collective-permute-start(bf16[192,384]{1,0:T(8,128)(2,1)S(1)} %get-tuple-element.145), channel_id=1, source_target_pairs={{0,64},{64,0},{128,192},{192,128},{1,65},{65,1},{129,193},{193,129... | collective-permute-start | bytes 442376 | tf_op jit(solution)/shard_map/ppermute | solution.py:32
  28.3 18.2 %collective-permute-start.8 = (bf16[160,1536]{1,0:T(8,128)(2,1)S(1)}, bf16[160,1536]{1,0:T(8,128)(2,1)S(1)}, u32[]{:S(2)}, u32[]{:S(2)}) collective-permute-start(bf16[160,1536]{1,0:T(8,128)(2,1)S(1)} %get-tuple-element.147), channel_id=1, source_target_pairs={{0,128},{128,0},{1,129},{129,1},{2,130},{130,2},{3,131},{131,3},{4... | collective-permute-start | bytes 1474568 | tf_op jit(solution)/shard_map/ppermute | solution.py:32
  34.3 16.8 %collective-permute-start.10 = (bf16[24,1536]{1,0:T(8,128)(2,1)S(1)}, bf16[24,1536]{1,0:T(8,128)(2,1)S(1)}, u32[]{:S(2)}, u32[]{:S(2)}) collective-permute-start(bf16[24,1536]{1,0:T(8,128)(2,1)S(1)} %pad_maximum_fusion.25), channel_id=1, source_target_pairs={{0,48},{16,32},{32,16},{48,0},{1,49},{17,33},{33,17},{49,1},{2,50}... | collective-permute-start | bytes 221192 | tf_op jit(solution)/shard_map/ppermute | solution.py:32
  37.3 14.3 %collective-permute-start.11 = (bf16[24,1536]{1,0:T(8,128)(2,1)S(1)}, bf16[24,1536]{1,0:T(8,128)(2,1)S(1)}, u32[]{:S(2)}, u32[]{:S(2)}) collective-permute-start(bf16[24,1536]{1,0:T(8,128)(2,1)S(1)} %pad_maximum_fusion.25), channel_id=1, source_target_pairs={{0,32},{16,48},{32,0},{48,16},{1,33},{17,49},{33,1},{49,17},{2,34}... | collective-permute-start | bytes 221192 | tf_op jit(solution)/shard_map/ppermute | solution.py:32
  39.1 12.5 %collective-permute-start.12 = (bf16[24,1536]{1,0:T(8,128)(2,1)S(1)}, bf16[24,1536]{1,0:T(8,128)(2,1)S(1)}, u32[]{:S(2)}, u32[]{:S(2)}) collective-permute-start(bf16[24,1536]{1,0:T(8,128)(2,1)S(1)} %pad_maximum_fusion.25), channel_id=1, source_target_pairs={{0,16},{16,0},{32,48},{48,32},{1,17},{17,1},{33,49},{49,33},{2,18}... | collective-permute-start | bytes 221192 | tf_op jit(solution)/shard_map/ppermute | solution.py:32
  46.6 7.7 %collective-permute-start.13 = (bf16[2,160,1536]{2,1,0:T(8,128)(2,1)S(1)}, bf16[2,160,1536]{2,1,0:T(8,128)(2,1)S(1)}, u32[]{:S(2)}, u32[]{:S(2)}) collective-permute-start(bf16[2,160,1536]{2,1,0:T(8,128)(2,1)S(1)} %pad_maximum_fusion.1), channel_id=1, source_target_pairs={{0,64},{64,0},{1,65},{65,1},{2,66},{66,2},{3,67},{67,3},{4,68},{68... | collective-permute-start | bytes 2949128 | tf_op jit(solution)/shard_map/ppermute | solution.py:32
  54.5 22.0 %collective-permute-start.17 = (bf16[4,24,1536]{2,1,0:T(8,128)(2,1)S(1)}, bf16[4,24,1536]{2,1,0:T(8,128)(2,1)S(1)}, u32[]{:S(2)}, u32[]{:S(2)}) collective-permute-start(bf16[4,24,1536]{2,1,0:T(8,128)(2,1)S(1)} %pad_maximum_fusion.10), channel_id=1, source_target_pairs={{0,12},{4,8},{8,4},{12,0},{1,13},{5,9},{9,5},{13,1},{2,14},{6,10},... | collective-permute-start | bytes 884744 | tf_op jit(solution)/shard_map/ppermute | solution.py:32
  58.3 18.2 %collective-permute-start.18 = (bf16[4,24,1536]{2,1,0:T(8,128)(2,1)S(1)}, bf16[4,24,1536]{2,1,0:T(8,128)(2,1)S(1)}, u32[]{:S(2)}, u32[]{:S(2)}) collective-permute-start(bf16[4,24,1536]{2,1,0:T(8,128)(2,1)S(1)} %pad_maximum_fusion.10), channel_id=1, source_target_pairs={{0,8},{4,12},{8,0},{12,4},{1,9},{5,13},{9,1},{13,5},{2,10},{6,14},... | collective-permute-start | bytes 884744 | tf_op jit(solution)/shard_map/ppermute | solution.py:32
  58.3 18.2 %collective-permute-start.19 = (bf16[4,24,1536]{2,1,0:T(8,128)(2,1)S(1)}, bf16[4,24,1536]{2,1,0:T(8,128)(2,1)S(1)}, u32[]{:S(2)}, u32[]{:S(2)}) collective-permute-start(bf16[4,24,1536]{2,1,0:T(8,128)(2,1)S(1)} %pad_maximum_fusion.10), channel_id=1, source_target_pairs={{0,4},{4,0},{8,12},{12,8},{1,5},{5,1},{9,13},{13,9},{2,6},{6,2},{1... | collective-permute-start | bytes 884744 | tf_op jit(solution)/shard_map/ppermute | solution.py:32
  59.0 4.6 %collective-permute-start.15 = (f32[3,384]{1,0:T(4,128)S(1)}, f32[3,384]{1,0:T(4,128)S(1)}, u32[]{:S(2)}, u32[]{:S(2)}) collective-permute-start(f32[3,384]{1,0:T(4,128)S(1)} %pad_maximum_fusion.29), channel_id=1, source_target_pairs={{0,16},{16,0},{32,48},{48,32},{1,17},{17,1},{33,49},{49,33},{2,18}... | collective-permute-start | bytes 13832 | tf_op jit(solution)/shard_map/ppermute | solution.py:32
  63.6 12.8 %collective-permute-start.16 = (f32[3,384]{1,0:T(4,128)S(1)}, f32[3,384]{1,0:T(4,128)S(1)}, u32[]{:S(2)}, u32[]{:S(2)}) collective-permute-start(f32[3,384]{1,0:T(4,128)S(1)} %pad_maximum_fusion.30), channel_id=1, source_target_pairs={{0,32},{16,48},{32,0},{48,16},{1,33},{17,49},{33,1},{49,17},{2,34}... | collective-permute-start | bytes 13832 | tf_op jit(solution)/shard_map/ppermute | solution.py:32
  94.1 20.9 %collective-permute-start.24 = (bf16[144,1536]{1,0:T(8,128)(2,1)S(1)}, bf16[144,1536]{1,0:T(8,128)(2,1)S(1)}, u32[]{:S(2)}, u32[]{:S(2)}) collective-permute-start(bf16[144,1536]{1,0:T(8,128)(2,1)S(1)} %get-tuple-element.199), channel_id=1, source_target_pairs={{0,12},{4,8},{8,4},{12,0},{1,13},{5,9},{9,5},{13,1},{2,14},{6,10},... | collective-permute-start | bytes 1327112 | tf_op jit(solution)/shard_map/ppermute | solution.py:32
  96.8 14.9 %collective-permute-start.23 = (bf16[144,1536]{1,0:T(8,128)(2,1)S(1)}, bf16[144,1536]{1,0:T(8,128)(2,1)S(1)}, u32[]{:S(2)}, u32[]{:S(2)}) collective-permute-start(bf16[144,1536]{1,0:T(8,128)(2,1)S(1)} %get-tuple-element.200), channel_id=1, source_target_pairs={{0,8},{4,12},{8,0},{12,4},{1,9},{5,13},{9,1},{13,5},{2,10},{6,14},... | collective-permute-start | bytes 1327112 | tf_op jit(solution)/shard_map/ppermute | solution.py:32
  96.8 14.9 %collective-permute-start.22 = (bf16[144,1536]{1,0:T(8,128)(2,1)S(1)}, bf16[144,1536]{1,0:T(8,128)(2,1)S(1)}, u32[]{:S(2)}, u32[]{:S(2)}) collective-permute-start(bf16[144,1536]{1,0:T(8,128)(2,1)S(1)} %get-tuple-element.198), channel_id=1, source_target_pairs={{0,4},{4,0},{8,12},{12,8},{1,5},{5,1},{9,13},{13,9},{2,6},{6,2},{1... | collective-permute-start | bytes 1327112 | tf_op jit(solution)/shard_map/ppermute | solution.py:32
  98.7 16.5 %collective-permute-start.25 = (bf16[2,128,1536]{2,1,0:T(8,128)(2,1)S(1)}, bf16[2,128,1536]{2,1,0:T(8,128)(2,1)S(1)}, u32[]{:S(2)}, u32[]{:S(2)}) collective-permute-start(bf16[2,128,1536]{2,1,0:T(8,128)(2,1)S(1)} %pad_maximum_fusion.2), channel_id=1, source_target_pairs={{0,64},{64,0},{1,65},{65,1},{2,66},{66,2},{3,67},{67,3},{4,68},{68... | collective-permute-start | bytes 2359304 | tf_op jit(solution)/shard_map/ppermute | solution.py:32
  115.5 6.7 %collective-permute-start.26 = (bf16[128,1536]{1,0:T(8,128)(2,1)S(1)}, bf16[128,1536]{1,0:T(8,128)(2,1)S(1)}, u32[]{:S(2)}, u32[]{:S(2)}) collective-permute-start(bf16[128,1536]{1,0:T(8,128)(2,1)S(1)} %fusion.3), channel_id=1, source_target_pairs={{0,128},{128,0},{1,129},{129,1},{2,130},{130,2},{3,131},{131,3},{4... | collective-permute-start | bytes 1179656 | tf_op jit(solution)/shard_map/ppermute | solution.py:32
  122.5 23.8 %collective-permute-start.29 = (bf16[72,1536]{1,0:T(8,128)(2,1)S(1)}, bf16[72,1536]{1,0:T(8,128)(2,1)S(1)}, u32[]{:S(2)}, u32[]{:S(2)}) collective-permute-start(bf16[72,1536]{1,0:T(8,128)(2,1)S(1)} %get-tuple-element.193), channel_id=1, source_target_pairs={{0,48},{16,32},{32,16},{48,0},{1,49},{17,33},{33,17},{49,1},{2,50}... | collective-permute-start | bytes 663560 | tf_op jit(solution)/shard_map/ppermute | solution.py:32
  127.0 19.3 %collective-permute-start.28 = (bf16[72,1536]{1,0:T(8,128)(2,1)S(1)}, bf16[72,1536]{1,0:T(8,128)(2,1)S(1)}, u32[]{:S(2)}, u32[]{:S(2)}) collective-permute-start(bf16[72,1536]{1,0:T(8,128)(2,1)S(1)} %get-tuple-element.192), channel_id=1, source_target_pairs={{0,32},{16,48},{32,0},{48,16},{1,33},{17,49},{33,1},{49,17},{2,34}... | collective-permute-start | bytes 663560 | tf_op jit(solution)/shard_map/ppermute | solution.py:32
  128.2 21.2 %collective-permute-start.27 = (bf16[72,1536]{1,0:T(8,128)(2,1)S(1)}, bf16[72,1536]{1,0:T(8,128)(2,1)S(1)}, u32[]{:S(2)}, u32[]{:S(2)}) collective-permute-start(bf16[72,1536]{1,0:T(8,128)(2,1)S(1)} %get-tuple-element.191), channel_id=1, source_target_pairs={{0,16},{16,0},{32,48},{48,32},{1,17},{17,1},{33,49},{49,33},{2,18}... | collective-permute-start | bytes 663560 | tf_op jit(solution)/shard_map/ppermute | solution.py:32
  149.7 5.5 %collective-permute-start.30 = (bf16[54,1536]{1,0:T(8,128)(2,1)S(1)}, bf16[54,1536]{1,0:T(8,128)(2,1)S(1)}, u32[]{:S(2)}, u32[]{:S(2)}) collective-permute-start(bf16[54,1536]{1,0:T(8,128)(2,1)S(1)} %get-tuple-element.186), channel_id=1, source_target_pairs={{0,1},{1,0},{2,3},{3,2},{4,5},{5,4},{6,7},{7,6},{8,9},{9,8},{10,11... | collective-permute-start | bytes 497672 | tf_op jit(solution)/shard_map/ppermute | solution.py:32
  150.1 9.4 %collective-permute-start.31 = (bf16[54,1536]{1,0:T(8,128)(2,1)S(1)}, bf16[54,1536]{1,0:T(8,128)(2,1)S(1)}, u32[]{:S(2)}, u32[]{:S(2)}) collective-permute-start(bf16[54,1536]{1,0:T(8,128)(2,1)S(1)} %get-tuple-element.185), channel_id=1, source_target_pairs={{0,2},{1,3},{2,0},{3,1},{4,6},{5,7},{6,4},{7,5},{8,10},{9,11},{10,... | collective-permute-start | bytes 497672 | tf_op jit(solution)/shard_map/ppermute | solution.py:32
  151.8 10.4 %collective-permute-start.32 = (bf16[54,1536]{1,0:T(8,128)(2,1)S(1)}, bf16[54,1536]{1,0:T(8,128)(2,1)S(1)}, u32[]{:S(2)}, u32[]{:S(2)}) collective-permute-start(bf16[54,1536]{1,0:T(8,128)(2,1)S(1)} %get-tuple-element.184), channel_id=1, source_target_pairs={{0,3},{1,2},{2,1},{3,0},{4,7},{5,6},{6,5},{7,4},{8,11},{9,10},{10,... | collective-permute-start | bytes 497672 | tf_op jit(solution)/shard_map/ppermute | solution.py:32
  166.9 6.2 %collective-permute-start.33 = (bf16[2,128,384]{2,1,0:T(8,128)(2,1)S(1)}, bf16[2,128,384]{2,1,0:T(8,128)(2,1)S(1)}, u32[]{:S(2)}, u32[]{:S(2)}) collective-permute-start(bf16[2,128,384]{2,1,0:T(8,128)(2,1)S(1)} %pad_maximum_fusion.15), channel_id=1, source_target_pairs={{0,64},{64,0},{1,65},{65,1},{2,66},{66,2},{3,67},{67,3},{4,68},{68... | collective-permute-start | bytes 589832 | tf_op jit(solution)/shard_map/ppermute | solution.py:32
  167.8 4.6 %collective-permute-start.36 = (f32[33,768]{1,0:T(8,128)S(1)}, f32[33,768]{1,0:T(8,128)S(1)}, u32[]{:S(2)}, u32[]{:S(2)}) collective-permute-start(f32[33,768]{1,0:T(8,128)S(1)} %pad_maximum_fusion.24), channel_id=1, source_target_pairs={{0,128},{128,0},{1,129},{129,1},{2,130},{130,2},{3,131},{131,3},{4... | collective-permute-start | bytes 304136 | tf_op jit(solution)/shard_map/ppermute | solution.py:32
  173.2 5.3 %collective-permute-start.34 = (bf16[2,128,384]{2,1,0:T(8,128)(2,1)S(1)}, bf16[2,128,384]{2,1,0:T(8,128)(2,1)S(1)}, u32[]{:S(2)}, u32[]{:S(2)}) collective-permute-start(bf16[2,128,384]{2,1,0:T(8,128)(2,1)S(1)} %pad_maximum_fusion.16), channel_id=1, source_target_pairs={{0,128},{128,0},{1,129},{129,1},{2,130},{130,2},{3,131},{131,3},{4... | collective-permute-start | bytes 589832 | tf_op jit(solution)/shard_map/ppermute | solution.py:32
  (22 other events, 182.5 us)

commit v2 on v1

--- a/solution.py
+++ b/solution.py
@@ -257,7 +257,6 @@
         (low, high, rows, lengths, kernel, gain, bias)
     )
     cot = jnp.concatenate([low[HALO:], cotangent, high[HALO:]], axis=0)
-    cot_z = swap(cot, "zl", 1)
     slab = jnp.concatenate([low[:HALO], glu_out, high[:HALO]], axis=0)
     pick = lambda m: lax.dynamic_slice_in_dim(slab, (dp ^ m) * own, own, axis=1)
     pieces = [pick(0)] + [swap(pick(m), DP, m) for m in (1, 2, 3)]
@@ -267,7 +266,7 @@
     limit = jnp.sum(jnp.where(places[None, :] == (dp ^ places)[:, None], lengths, 0), axis=1)
     meta = jnp.concatenate([limit, jnp.stack([seq, total])])
 
-    rows, pieces[2] = barrier((rows, pieces[2]))
+    rows, pieces[1] = barrier((rows, pieces[1]))
     rows = jnp.concatenate(in_order(lax.axis_index("x"), rows), axis=0)
     rows = jnp.stack(in_order(lax.axis_index("zh"), exchange(rows, "zh")), axis=0)
     slabs = jnp.stack(pieces)
@@ -291,11 +290,12 @@
         meta=meta,
     )
     mean = stats[1:2]
-    stats, cot_z, affine = barrier((stats, cot_z, affine))
-
+    stats, cot, affine, rows = barrier((stats, cot, affine, rows))
+
+    cot_z = swap(cot, "zl", 1)
     pair = swap(jnp.stack([cot, cot_z]), "core", 1)
     stats = combine(stats, *STAGES[0])
-    stats, rows, mean, pair = barrier((stats, rows, mean, pair))
+    stats, rows, mean = barrier((stats, rows, mean))
     rows = jnp.stack(in_order(lax.axis_index("y"), exchange(rows, "y")), axis=1).reshape(own, width)
     grad_out = jnp.stack([cot, pair[0], cot_z, pair[1]])
     grad_out = jnp.where(valid_rows(EDGE), grad_out, jnp.zeros((), bf16))
@@ -342,9 +342,9 @@
     weight_grad, sums = scatter_stage(weight_grad, sums, "y", 1)
     other = swap(jnp.stack([product[1], product[3]]).astype(bf16), "core", 1).astype(f32)
     kept, far = product[0] + other[0], product[2] + other[1]
+    weight_grad, sums = scatter_stage(weight_grad, sums, "zh", 0)
+    sums, far = barrier((sums, far))
     product = kept + swap(far.astype(bf16), "zl", 1).astype(f32)
-    weight_grad, sums, product = barrier((weight_grad, sums, product))
-    weight_grad, sums = scatter_stage(weight_grad, sums, "zh", 0)
     weight_grad, sums = scatter_stage(weight_grad.reshape(4, own // 64, width), sums, "x", 0)
     stream_valid = (seq * frames + jnp.arange(frames, dtype=jnp.int32) < limit[0])[:, None]
     module_out = jnp.where(stream_valid, product, 0.0).astype(bf16)
@@ -356,14 +356,14 @@
         [pltpu.VMEM((4, span, LANES), f32)],
         meta=meta,
     )
-    _, sums = barrier((flipped, sums))
+    near = swap(jnp.stack([flipped[1], flipped[3]]), "core", 1)
+    near, sums = barrier((near, sums))
     gain_grad, bias_grad = sums[KERNEL : KERNEL + 1], sums[KERNEL + 1 : KERNEL + 2]
     tap_in, tap_off = sums[KERNEL + 3 : 2 * KERNEL + 3], sums[2 * KERNEL + 3 :]
     tap_sums = (inv_std * gain_own) * (
         sums[:KERNEL] - bias_grad / count * tap_in - gain_grad / count * tap_off
     )
     table = jnp.concatenate([tap_sums, sums[KERNEL : KERNEL + 2]], axis=0)
-    near = swap(jnp.stack([flipped[1], flipped[3]]), "core", 1)
     far = swap(jnp.stack([flipped[2], near[1]]), "zl", 1)
     input_grad = jnp.concatenate(in_order(dp, [flipped[0], near[0], far[0], far[1]]), axis=1)
     table = side_by_side(side_by_side(table, "core"), "zl")

time: 182 us -> 167 us (0.918); the launches traced: 179 us -> 166 us
  waiting for transfers between devices: 73.7 us -> 54.8 us
  other arithmetic: 8.45 us -> 10.7 us
    ppermute x35, waiting for transfers between devices: 68.2 us -> 54.2 us  [swap(): return lax.ppermute(value, axis, [(i, i ^ mask) for i in range(size(axis))])]
    ppermute x2, waiting for transfers between devices: 5.46 us -> 0.58 us  [shift(): lax.ppermute(value, axis, [(i, (i + step) % count) for i in range(count)])]
    add x12, other arithmetic: 0.28 us -> 2.76 us  [whole_again(): return jnp.concatenate([parts[0] + parts[2], parts[1] + parts[3]], axis=0)]
    unnamed x32 -> x38, local copies, waits for them, and re-layouts: 2.22 us -> 4.52 us
  transfers between devices with their start and end apart: 37 -> 37, of which waited for: 21 -> 23; matrix products, arithmetic and copies ran while one was open for 5% -> 6% of each run, Pallas kernels for 5% -> 7%
where the time goes in v2:
time: 167 us; the launch traced here: 166 us
  starting transfers between devices  68.3 us (41%)
  waiting for transfers between devices  54.8 us (33%)
  Pallas kernels  14.9 us (9%)
  other arithmetic  10.7 us (6%)
  local copies, waits for them, and re-layouts  8.45 us (5%)
  matrix products  6.98 us (4%)
  between operations  2.12 us (1%)
    ppermute x35, starting transfers between devices, swap(): return lax.ppermute(value, axis, [(i, i ^ mask) for i in range(size(axis))])  56.6 us
    ppermute x35, waiting for transfers between devices, swap(): return lax.ppermute(value, axis, [(i, i ^ mask) for i in range(size(axis))])  54.2 us
    pallas_call x4, Pallas kernels, by_lanes(): pl.pallas_call(kernel, out_shape=shapes, grid_spec=pltpu.PrefetchScalarGr...  14.9 us
    ppermute x2, starting transfers between devices, shift(): lax.ppermute(value, axis, [(i, (i + step) % count) for i in range(count)])  11.7 us
    unnamed x38, local copies, waits for them, and re-layouts  4.52 us
  transfers between devices with their start and end apart: 37, of which 23 were waited for; matrix products, arithmetic and copies ran while one was open for 6% of the time, Pallas kernels for 7%

profile of v2, /device:TPU:1, one launch (start us, length us, event | category | flops | bytes accessed | tf_op | source)
XLA Modules:
  0.0 166.2 jit_solution(11743813881241732908)
XLA Ops:
  2.6 2.1 %collective-permute-start = (bf16[48,1536]{1,0:T(8,128)(2,1)S(1)}, bf16[48,1536]{1,0:T(8,128)(2,1)S(1)}, u32[]{:S(2)}, u32[]{:S(2)}) collective-permute-start(bf16[48,1536]{1,0:T(8,128)(2,1)S(1)} %get-tuple-element.52), channel_id=1, source_target_pairs={{0,1},{1,2},{2,3},{3,4},{4,5},{5,6},{6,7},{7,8},{8,9},{9,10},{10,1... | collective-permute-start | bytes 442376 | tf_op jit(solution)/shard_map/ppermute | solution.py:37
  4.7 9.5 %collective-permute-start.1 = (bf16[48,1536]{1,0:T(8,128)(2,1)S(1)}, bf16[48,1536]{1,0:T(8,128)(2,1)S(1)}, u32[]{:S(2)}, u32[]{:S(2)}) collective-permute-start(bf16[48,1536]{1,0:T(8,128)(2,1)S(1)} %get-tuple-element.53), channel_id=1, source_target_pairs={{0,63},{1,0},{2,1},{3,2},{4,3},{5,4},{6,5},{7,6},{8,7},{9,8},{10,9... | collective-permute-start | bytes 442376 | tf_op jit(solution)/shard_map/ppermute | solution.py:37
  14.2 3.2 %collective-permute-start.2 = (bf16[6,1536]{1,0:T(8,128)(2,1)}, bf16[6,1536]{1,0:T(8,128)(2,1)S(1)}, u32[]{:S(2)}, u32[]{:S(2)}) collective-permute-start(bf16[6,1536]{1,0:T(8,128)(2,1)} %param.15), channel_id=1, source_target_pairs={{0,1},{1,0},{2,3},{3,2},{4,5},{5,4},{6,7},{7,6},{8,9},{9,8},{10,11... | collective-permute-start | bytes 55304 | tf_op jit(solution)/shard_map/ppermute | solution.py:32
  21.1 2.8 %collective-permute-start.7 = (bf16[192,384]{1,0:T(8,128)(2,1)S(1)}, bf16[192,384]{1,0:T(8,128)(2,1)S(1)}, u32[]{:S(2)}, u32[]{:S(2)}) collective-permute-start(bf16[192,384]{1,0:T(8,128)(2,1)S(1)} %get-tuple-element.143), channel_id=1, source_target_pairs={{0,192},{64,128},{128,64},{192,0},{1,193},{65,129},{129,65},{193,1... | collective-permute-start | bytes 442376 | tf_op jit(solution)/shard_map/ppermute | solution.py:32
  25.6 4.6 %collective-permute-start.9 = (bf16[24,1536]{1,0:T(8,128)(2,1)S(1)}, bf16[24,1536]{1,0:T(8,128)(2,1)S(1)}, u32[]{:S(2)}, u32[]{:S(2)}) collective-permute-start(bf16[24,1536]{1,0:T(8,128)(2,1)S(1)} %pad_maximum_fusion.25), channel_id=1, source_target_pairs={{0,32},{16,48},{32,0},{48,16},{1,33},{17,49},{33,1},{49,17},{2,34}... | collective-permute-start | bytes 221192 | tf_op jit(solution)/shard_map/ppermute | solution.py:32
  31.3 1.8 %collective-permute-done.6 = bf16[192,384]{1,0:T(8,128)(2,1)S(1)} collective-permute-done((bf16[192,384]{1,0:T(8,128)(2,1)S(1)}, bf16[192,384]{1,0:T(8,128)(2,1)S(1)}, u32[]{:S(2)}, u32[]{:S(2)}) %collective-permute-start.6) | collective-permute-done | bytes 147488 | tf_op jit(solution)/shard_map/ppermute | solution.py:32
  33.2 3.5 %shard_map.161 = (f32[4,192,384]{2,1,0:T(8,128)S(1)}, f32[4,160,384]{2,1,0:T(8,128)S(1)}, f32[3,384]{1,0:T(4,128)S(1)}) custom-call(s32[6]{0:T(128)S(1)} %pad_add_fusion.meta_ref, bf16[4,192,384]{2,1,0:T(8,128)(2,1)S(1)} %pad_maximum_fusion.4.slab_ref, f32[31,384]{1,0:T(8,128)S(1)} %constant_dynamic-slice_fusion.taps_ref), custom_call_target="tpu_custom_call" | custom-call | tf_op jit(solution)/shard_map/pallas_call | solution.py:228
  36.7 3.3 %collective-permute-done.9 = bf16[24,1536]{1,0:T(8,128)(2,1)S(1)} collective-permute-done((bf16[24,1536]{1,0:T(8,128)(2,1)S(1)}, bf16[24,1536]{1,0:T(8,128)(2,1)S(1)}, u32[]{:S(2)}, u32[]{:S(2)}) %collective-permute-start.9) | collective-permute-done | bytes 73760 | tf_op jit(solution)/shard_map/ppermute | solution.py:32
  40.9 1.8 %collective-permute-done.11 = f32[3,384]{1,0:T(4,128)S(1)} collective-permute-done((f32[3,384]{1,0:T(4,128)S(1)}, f32[3,384]{1,0:T(4,128)S(1)}, u32[]{:S(2)}, u32[]{:S(2)}) %collective-permute-start.11) | collective-permute-done | bytes 4640 | tf_op jit(solution)/shard_map/ppermute | solution.py:32
  42.8 2.0 %collective-permute-start.12 = (f32[3,384]{1,0:T(4,128)S(1)}, f32[3,384]{1,0:T(4,128)S(1)}, u32[]{:S(2)}, u32[]{:S(2)}) collective-permute-start(f32[3,384]{1,0:T(4,128)S(1)} %pad_maximum_fusion.28), channel_id=1, source_target_pairs={{0,2},{1,3},{2,0},{3,1},{4,6},{5,7},{6,4},{7,5},{8,10},{9,11},{10,... | collective-permute-start | bytes 13832 | tf_op jit(solution)/shard_map/ppermute | solution.py:32
  46.9 2.9 %collective-permute-start.13 = (f32[3,384]{1,0:T(4,128)S(1)}, f32[3,384]{1,0:T(4,128)S(1)}, u32[]{:S(2)}, u32[]{:S(2)}) collective-permute-start(f32[3,384]{1,0:T(4,128)S(1)} %pad_maximum_fusion.29), channel_id=1, source_target_pairs={{0,16},{16,0},{32,48},{48,32},{1,17},{17,1},{33,49},{49,33},{2,18}... | collective-permute-start | bytes 13832 | tf_op jit(solution)/shard_map/ppermute | solution.py:32
  49.9 3.6 %collective-permute-start.18 = (bf16[4,24,1536]{2,1,0:T(8,128)(2,1)S(1)}, bf16[4,24,1536]{2,1,0:T(8,128)(2,1)S(1)}, u32[]{:S(2)}, u32[]{:S(2)}) collective-permute-start(bf16[4,24,1536]{2,1,0:T(8,128)(2,1)S(1)} %pad_maximum_fusion.10), channel_id=1, source_target_pairs={{0,8},{4,12},{8,0},{12,4},{1,9},{5,13},{9,1},{13,5},{2,10},{6,14},... | collective-permute-start | bytes 884744 | tf_op jit(solution)/shard_map/ppermute | solution.py:32
  53.8 4.9 %shard_map.162 = (f32[31,384]{1,0:T(8,128)S(1)}, f32[31,384]{1,0:T(8,128)S(1)}) custom-call(s32[6]{0:T(128)S(1)} %pad_add_fusion.meta_ref, f32[4,192,384]{2,1,0:T(8,128)S(1)} %get-tuple-element.79.masked_ref, f32[4,160,384]{2,1,0:T(8,128)S(1)} %get-tuple-element.66.conv_ref, f32[1,384]{1,0:T(1,128)S(1)} %slice.500.mean_ref), custom_call_target="tpu_custom_call" | custom-call | tf_op jit(solution)/shard_map/pallas_call | solution.py:228
  60.4 4.3 %collective-permute-start.16 = (bf16[2,160,1536]{2,1,0:T(8,128)(2,1)S(1)}, bf16[2,160,1536]{2,1,0:T(8,128)(2,1)S(1)}, u32[]{:S(2)}, u32[]{:S(2)}) collective-permute-start(bf16[2,160,1536]{2,1,0:T(8,128)(2,1)S(1)} %pad_maximum_fusion.1), channel_id=1, source_target_pairs={{0,64},{64,0},{1,65},{65,1},{2,66},{66,2},{3,67},{67,3},{4,68},{68... | collective-permute-start | bytes 2949128 | tf_op jit(solution)/shard_map/ppermute | solution.py:32
  65.3 2.7 %collective-permute-done.17 = bf16[4,24,1536]{2,1,0:T(8,128)(2,1)S(1)} collective-permute-done((bf16[4,24,1536]{2,1,0:T(8,128)(2,1)S(1)}, bf16[4,24,1536]{2,1,0:T(8,128)(2,1)S(1)}, u32[]{:S(2)}, u32[]{:S(2)}) %collective-permute-start.17) | collective-permute-done | bytes 294944 | tf_op jit(solution)/shard_map/ppermute | solution.py:32
  70.1 2.2 %fusion.57.back_ref = f32[4,160,384]{2,1,0:T(8,128)} fusion(bf16[4,160,1536]{2,1,0:T(8,128)(2,1)S(1)} %maximum_select_fusion, bf16[384,1536,1]{1,0,2:T(8,128)(2,1)S(1)} %bitcast.124), kind=kOutput, calls=%fused_computation.242 | convolution fusion | flops 754974720 | bytes 4128768 | tf_op jit(solution)/shard_map/dot_general | solution.py:302
  72.2 2.5 %collective-permute-done.20 = f32[3,384]{1,0:T(4,128)S(1)} collective-permute-done((f32[3,384]{1,0:T(4,128)S(1)}, f32[3,384]{1,0:T(4,128)S(1)}, u32[]{:S(2)}, u32[]{:S(2)}) %collective-permute-start.20) | collective-permute-done | bytes 4640 | tf_op jit(solution)/shard_map/ppermute | solution.py:32
  75.7 3.1 %collective-permute-done.21 = f32[3,384]{1,0:T(4,128)S(1)} collective-permute-done((f32[3,384]{1,0:T(4,128)S(1)}, f32[3,384]{1,0:T(4,128)S(1)}, u32[]{:S(2)}, u32[]{:S(2)}) %collective-permute-start.21) | collective-permute-done | bytes 4640 | tf_op jit(solution)/shard_map/ppermute | solution.py:32
  80.1 3.5 %shard_map.163 = (bf16[4,128,384]{2,1,0:T(8,128)(2,1)S(1)}, f32[4,160,384]{2,1,0:T(8,128)S(1)}, f32[34,384]{1,0:T(8,128)S(1)}) custom-call(s32[6]{0:T(128)S(1)} %pad_add_fusion.meta_ref, f32[4,160,384]{2,1,0:T(8,128)S(1)} %get-tuple-element.66.conv_ref, f32[4,160,384]{2,1,0:T(8,128)S(1)} %copy-done.1, f32[4,192,384]{2,1,0:T(8,128)S(1)} %get-tuple-element.79.masked_ref, ...), custom_call_target="tpu_custom_call" | custom-call | tf_op jit(solution)/shard_map/pallas_call | solution.py:228
  84.8 2.2 %fusion = f32[4,4,24,1536]{3,2,1,0:T(8,128)S(1)} fusion(bf16[4,4,24,512]{3,2,1,0:T(8,128)(2,1)S(1)} %bitcast.131, bf16[512,1536]{1,0:T(8,128)(2,1)} %bitcast.123), kind=kOutput, calls=%fused_computation.1 | convolution fusion | flops 603979776 | bytes 4325376 | tf_op jit(solution)/shard_map/dot_general | solution.py:334
  88.0 2.7 %collective-permute-start.24 = (bf16[144,1536]{1,0:T(8,128)(2,1)S(1)}, bf16[144,1536]{1,0:T(8,128)(2,1)S(1)}, u32[]{:S(2)}, u32[]{:S(2)}) collective-permute-start(bf16[144,1536]{1,0:T(8,128)(2,1)S(1)} %get-tuple-element.198), channel_id=1, source_target_pairs={{0,8},{4,12},{8,0},{12,4},{1,9},{5,13},{9,1},{13,5},{2,10},{6,14},... | collective-permute-start | bytes 1327112 | tf_op jit(solution)/shard_map/ppermute | solution.py:32
  90.6 2.6 %fusion.56 = (bf16[512,1536]{1,0:T(8,128)(2,1)S(1)}, f32[512,1536]{1,0:T(8,128)}) fusion(bf16[512,384]{1,0:T(8,128)(2,1)S(1)} %bitcast.122, bf16[384,1536]{1,0:T(8,128)(2,1)S(1)} %bitcast.125), kind=kOutput, calls=%fused_computation.241 | convolution fusion | flops 604766208 | bytes 6291456 | tf_op jit(solution)/shard_map/dot_general | solution.py:340
  93.4 5.7 %collective-permute-start.22 = (bf16[2,128,1536]{2,1,0:T(8,128)(2,1)S(1)}, bf16[2,128,1536]{2,1,0:T(8,128)(2,1)S(1)}, u32[]{:S(2)}, u32[]{:S(2)}) collective-permute-start(bf16[2,128,1536]{2,1,0:T(8,128)(2,1)S(1)} %pad_maximum_fusion.2), channel_id=1, source_target_pairs={{0,64},{64,0},{1,65},{65,1},{2,66},{66,2},{3,67},{67,3},{4,68},{68... | collective-permute-start | bytes 2359304 | tf_op jit(solution)/shard_map/ppermute | solution.py:32
  102.9 2.8 %collective-permute-start.28 = (bf16[72,1536]{1,0:T(8,128)(2,1)S(1)}, bf16[72,1536]{1,0:T(8,128)(2,1)S(1)}, u32[]{:S(2)}, u32[]{:S(2)}) collective-permute-start(bf16[72,1536]{1,0:T(8,128)(2,1)S(1)} %get-tuple-element.189), channel_id=1, source_target_pairs={{0,48},{16,32},{32,16},{48,0},{1,49},{17,33},{33,17},{49,1},{2,50}... | collective-permute-start | bytes 663560 | tf_op jit(solution)/shard_map/ppermute | solution.py:32
  105.7 4.0 %collective-permute-start.27 = (bf16[72,1536]{1,0:T(8,128)(2,1)S(1)}, bf16[72,1536]{1,0:T(8,128)(2,1)S(1)}, u32[]{:S(2)}, u32[]{:S(2)}) collective-permute-start(bf16[72,1536]{1,0:T(8,128)(2,1)S(1)} %get-tuple-element.190), channel_id=1, source_target_pairs={{0,32},{16,48},{32,0},{48,16},{1,33},{17,49},{33,1},{49,17},{2,34}... | collective-permute-start | bytes 663560 | tf_op jit(solution)/shard_map/ppermute | solution.py:32
  111.3 4.3 %collective-permute-done.27 = bf16[72,1536]{1,0:T(8,128)(2,1)S(1)} collective-permute-done((bf16[72,1536]{1,0:T(8,128)(2,1)S(1)}, bf16[72,1536]{1,0:T(8,128)(2,1)S(1)}, u32[]{:S(2)}, u32[]{:S(2)}) %collective-permute-start.27) | collective-permute-done | bytes 221216 | tf_op jit(solution)/shard_map/ppermute | solution.py:32
  115.6 11.4 %collective-permute-done.26 = bf16[72,1536]{1,0:T(8,128)(2,1)S(1)} collective-permute-done((bf16[72,1536]{1,0:T(8,128)(2,1)S(1)}, bf16[72,1536]{1,0:T(8,128)(2,1)S(1)}, u32[]{:S(2)}, u32[]{:S(2)}) %collective-permute-start.26) | collective-permute-done | bytes 221216 | tf_op jit(solution)/shard_map/ppermute | solution.py:32
  132.4 7.8 %collective-permute-start.32 = (bf16[54,1536]{1,0:T(8,128)(2,1)S(1)}, bf16[54,1536]{1,0:T(8,128)(2,1)S(1)}, u32[]{:S(2)}, u32[]{:S(2)}) collective-permute-start(bf16[54,1536]{1,0:T(8,128)(2,1)S(1)} %get-tuple-element.182), channel_id=1, source_target_pairs={{0,3},{1,2},{2,1},{3,0},{4,7},{5,6},{6,5},{7,4},{8,11},{9,10},{10,... | collective-permute-start | bytes 497672 | tf_op jit(solution)/shard_map/ppermute | solution.py:32
  140.8 6.7 %collective-permute-done.32 = bf16[54,1536]{1,0:T(8,128)(2,1)S(1)} collective-permute-done((bf16[54,1536]{1,0:T(8,128)(2,1)S(1)}, bf16[54,1536]{1,0:T(8,128)(2,1)S(1)}, u32[]{:S(2)}, u32[]{:S(2)}) %collective-permute-start.32) | collective-permute-done | bytes 165920 | tf_op jit(solution)/shard_map/ppermute | solution.py:32
  148.5 3.0 %shard_map.164 = bf16[4,128,384]{2,1,0:T(8,128)(2,1)S(1)} custom-call(s32[6]{0:T(128)S(1)} %pad_add_fusion.meta_ref, f32[4,160,384]{2,1,0:T(8,128)S(1)} %get-tuple-element.66.conv_ref, f32[4,160,384]{2,1,0:T(8,128)S(1)} %copy-done.3, f32[3,384]{1,0:T(4,128)S(1)} %pad_maximum_fusion.33.stats_ref, f32[2,384]{1,0:T(2,128)S(1)} %fusion.31.affine_ref, ...), custom_call_target="tpu_custom_call" | custom-call | tf_op jit(solution)/shard_map/pallas_call | solution.py:228
  151.6 1.7 %collective-permute-start.33 = (bf16[2,128,384]{2,1,0:T(8,128)(2,1)S(1)}, bf16[2,128,384]{2,1,0:T(8,128)(2,1)S(1)}, u32[]{:S(2)}, u32[]{:S(2)}) collective-permute-start(bf16[2,128,384]{2,1,0:T(8,128)(2,1)S(1)} %pad_maximum_fusion.15), channel_id=1, source_target_pairs={{0,64},{64,0},{1,65},{65,1},{2,66},{66,2},{3,67},{67,3},{4,68},{68... | collective-permute-start | bytes 589832 | tf_op jit(solution)/shard_map/ppermute | solution.py:32
  157.5 6.5 %collective-permute-done.36 = f32[33,768]{1,0:T(8,128)S(1)} collective-permute-done((f32[33,768]{1,0:T(8,128)S(1)}, f32[33,768]{1,0:T(8,128)S(1)}, u32[]{:S(2)}, u32[]{:S(2)}) %collective-permute-start.36) | collective-permute-done | bytes 101408 | tf_op jit(solution)/shard_map/ppermute | solution.py:32
  (194 shorter events, 38.5 us)
Async XLA Ops:
  2.6 16.9 %collective-permute-start = (bf16[48,1536]{1,0:T(8,128)(2,1)S(1)}, bf16[48,1536]{1,0:T(8,128)(2,1)S(1)}, u32[]{:S(2)}, u32[]{:S(2)}) collective-permute-start(bf16[48,1536]{1,0:T(8,128)(2,1)S(1)} %get-tuple-element.52), channel_id=1, source_target_pairs={{0,1},{1,2},{2,3},{3,4},{4,5},{5,6},{6,7},{7,8},{8,9},{9,10},{10,1... | collective-permute-start | bytes 442376 | tf_op jit(solution)/shard_map/ppermute | solution.py:37
  4.7 15.4 %collective-permute-start.1 = (bf16[48,1536]{1,0:T(8,128)(2,1)S(1)}, bf16[48,1536]{1,0:T(8,128)(2,1)S(1)}, u32[]{:S(2)}, u32[]{:S(2)}) collective-permute-start(bf16[48,1536]{1,0:T(8,128)(2,1)S(1)} %get-tuple-element.53), channel_id=1, source_target_pairs={{0,63},{1,0},{2,1},{3,2},{4,3},{5,4},{6,5},{7,6},{8,7},{9,8},{10,9... | collective-permute-start | bytes 442376 | tf_op jit(solution)/shard_map/ppermute | solution.py:37
  14.2 4.4 %collective-permute-start.4 = (bf16[6,1536]{1,0:T(8,128)(2,1)}, bf16[6,1536]{1,0:T(8,128)(2,1)S(1)}, u32[]{:S(2)}, u32[]{:S(2)}) collective-permute-start(bf16[6,1536]{1,0:T(8,128)(2,1)} %param.15), channel_id=1, source_target_pairs={{0,3},{1,2},{2,1},{3,0},{4,7},{5,6},{6,5},{7,4},{8,11},{9,10},{10,... | collective-permute-start | bytes 55304 | tf_op jit(solution)/shard_map/ppermute | solution.py:32
  14.2 4.7 %collective-permute-start.3 = (bf16[6,1536]{1,0:T(8,128)(2,1)}, bf16[6,1536]{1,0:T(8,128)(2,1)S(1)}, u32[]{:S(2)}, u32[]{:S(2)}) collective-permute-start(bf16[6,1536]{1,0:T(8,128)(2,1)} %param.15), channel_id=1, source_target_pairs={{0,2},{1,3},{2,0},{3,1},{4,6},{5,7},{6,4},{7,5},{8,10},{9,11},{10,... | collective-permute-start | bytes 55304 | tf_op jit(solution)/shard_map/ppermute | solution.py:32
  14.2 5.2 %collective-permute-start.2 = (bf16[6,1536]{1,0:T(8,128)(2,1)}, bf16[6,1536]{1,0:T(8,128)(2,1)S(1)}, u32[]{:S(2)}, u32[]{:S(2)}) collective-permute-start(bf16[6,1536]{1,0:T(8,128)(2,1)} %param.15), channel_id=1, source_target_pairs={{0,1},{1,0},{2,3},{3,2},{4,5},{5,4},{6,7},{7,6},{8,9},{9,8},{10,11... | collective-permute-start | bytes 55304 | tf_op jit(solution)/shard_map/ppermute | solution.py:32
  21.1 10.2 %collective-permute-start.7 = (bf16[192,384]{1,0:T(8,128)(2,1)S(1)}, bf16[192,384]{1,0:T(8,128)(2,1)S(1)}, u32[]{:S(2)}, u32[]{:S(2)}) collective-permute-start(bf16[192,384]{1,0:T(8,128)(2,1)S(1)} %get-tuple-element.143), channel_id=1, source_target_pairs={{0,192},{64,128},{128,64},{192,0},{1,193},{65,129},{129,65},{193,1... | collective-permute-start | bytes 442376 | tf_op jit(solution)/shard_map/ppermute | solution.py:32
  23.9 9.2 %collective-permute-start.6 = (bf16[192,384]{1,0:T(8,128)(2,1)S(1)}, bf16[192,384]{1,0:T(8,128)(2,1)S(1)}, u32[]{:S(2)}, u32[]{:S(2)}) collective-permute-start(bf16[192,384]{1,0:T(8,128)(2,1)S(1)} %get-tuple-element.144), channel_id=1, source_target_pairs={{0,128},{64,192},{128,0},{192,64},{1,129},{65,193},{129,1},{193,65... | collective-permute-start | bytes 442376 | tf_op jit(solution)/shard_map/ppermute | solution.py:32
  25.5 11.2 %collective-permute-start.10 = (bf16[24,1536]{1,0:T(8,128)(2,1)S(1)}, bf16[24,1536]{1,0:T(8,128)(2,1)S(1)}, u32[]{:S(2)}, u32[]{:S(2)}) collective-permute-start(bf16[24,1536]{1,0:T(8,128)(2,1)S(1)} %pad_maximum_fusion.25), channel_id=1, source_target_pairs={{0,16},{16,0},{32,48},{48,32},{1,17},{17,1},{33,49},{49,33},{2,18}... | collective-permute-start | bytes 221192 | tf_op jit(solution)/shard_map/ppermute | solution.py:32
  25.6 14.4 %collective-permute-start.9 = (bf16[24,1536]{1,0:T(8,128)(2,1)S(1)}, bf16[24,1536]{1,0:T(8,128)(2,1)S(1)}, u32[]{:S(2)}, u32[]{:S(2)}) collective-permute-start(bf16[24,1536]{1,0:T(8,128)(2,1)S(1)} %pad_maximum_fusion.25), channel_id=1, source_target_pairs={{0,32},{16,48},{32,0},{48,16},{1,33},{17,49},{33,1},{49,17},{2,34}... | collective-permute-start | bytes 221192 | tf_op jit(solution)/shard_map/ppermute | solution.py:32
  30.2 9.8 %collective-permute-start.8 = (bf16[24,1536]{1,0:T(8,128)(2,1)S(1)}, bf16[24,1536]{1,0:T(8,128)(2,1)S(1)}, u32[]{:S(2)}, u32[]{:S(2)}) collective-permute-start(bf16[24,1536]{1,0:T(8,128)(2,1)S(1)} %pad_maximum_fusion.25), channel_id=1, source_target_pairs={{0,48},{16,32},{32,16},{48,0},{1,49},{17,33},{33,17},{49,1},{2,50}... | collective-permute-start | bytes 221192 | tf_op jit(solution)/shard_map/ppermute | solution.py:32
  42.8 4.1 %collective-permute-start.12 = (f32[3,384]{1,0:T(4,128)S(1)}, f32[3,384]{1,0:T(4,128)S(1)}, u32[]{:S(2)}, u32[]{:S(2)}) collective-permute-start(f32[3,384]{1,0:T(4,128)S(1)} %pad_maximum_fusion.28), channel_id=1, source_target_pairs={{0,2},{1,3},{2,0},{3,1},{4,6},{5,7},{6,4},{7,5},{8,10},{9,11},{10,... | collective-permute-start | bytes 13832 | tf_op jit(solution)/shard_map/ppermute | solution.py:32
  44.8 15.5 %collective-permute-start.15 = (bf16[160,1536]{1,0:T(8,128)(2,1)S(1)}, bf16[160,1536]{1,0:T(8,128)(2,1)S(1)}, u32[]{:S(2)}, u32[]{:S(2)}) collective-permute-start(bf16[160,1536]{1,0:T(8,128)(2,1)S(1)} %pad_maximum_fusion.5), channel_id=1, source_target_pairs={{0,128},{128,0},{1,129},{129,1},{2,130},{130,2},{3,131},{131,3},{4... | collective-permute-start | bytes 1474568 | tf_op jit(solution)/shard_map/ppermute | solution.py:32
  46.9 11.8 %collective-permute-start.13 = (f32[3,384]{1,0:T(4,128)S(1)}, f32[3,384]{1,0:T(4,128)S(1)}, u32[]{:S(2)}, u32[]{:S(2)}) collective-permute-start(f32[3,384]{1,0:T(4,128)S(1)} %pad_maximum_fusion.29), channel_id=1, source_target_pairs={{0,16},{16,0},{32,48},{48,32},{1,17},{17,1},{33,49},{49,33},{2,18}... | collective-permute-start | bytes 13832 | tf_op jit(solution)/shard_map/ppermute | solution.py:32
  49.9 15.3 %collective-permute-start.19 = (bf16[4,24,1536]{2,1,0:T(8,128)(2,1)S(1)}, bf16[4,24,1536]{2,1,0:T(8,128)(2,1)S(1)}, u32[]{:S(2)}, u32[]{:S(2)}) collective-permute-start(bf16[4,24,1536]{2,1,0:T(8,128)(2,1)S(1)} %pad_maximum_fusion.10), channel_id=1, source_target_pairs={{0,4},{4,0},{8,12},{12,8},{1,5},{5,1},{9,13},{13,9},{2,6},{6,2},{1... | collective-permute-start | bytes 884744 | tf_op jit(solution)/shard_map/ppermute | solution.py:32
  49.9 15.3 %collective-permute-start.18 = (bf16[4,24,1536]{2,1,0:T(8,128)(2,1)S(1)}, bf16[4,24,1536]{2,1,0:T(8,128)(2,1)S(1)}, u32[]{:S(2)}, u32[]{:S(2)}) collective-permute-start(bf16[4,24,1536]{2,1,0:T(8,128)(2,1)S(1)} %pad_maximum_fusion.10), channel_id=1, source_target_pairs={{0,8},{4,12},{8,0},{12,4},{1,9},{5,13},{9,1},{13,5},{2,10},{6,14},... | collective-permute-start | bytes 884744 | tf_op jit(solution)/shard_map/ppermute | solution.py:32
  53.5 14.4 %collective-permute-start.17 = (bf16[4,24,1536]{2,1,0:T(8,128)(2,1)S(1)}, bf16[4,24,1536]{2,1,0:T(8,128)(2,1)S(1)}, u32[]{:S(2)}, u32[]{:S(2)}) collective-permute-start(bf16[4,24,1536]{2,1,0:T(8,128)(2,1)S(1)} %pad_maximum_fusion.10), channel_id=1, source_target_pairs={{0,12},{4,8},{8,4},{12,0},{1,13},{5,9},{9,5},{13,1},{2,14},{6,10},... | collective-permute-start | bytes 884744 | tf_op jit(solution)/shard_map/ppermute | solution.py:32
  58.7 6.5 %collective-permute-start.14 = (f32[3,384]{1,0:T(4,128)S(1)}, f32[3,384]{1,0:T(4,128)S(1)}, u32[]{:S(2)}, u32[]{:S(2)}) collective-permute-start(f32[3,384]{1,0:T(4,128)S(1)} %pad_maximum_fusion.30), channel_id=1, source_target_pairs={{0,32},{16,48},{32,0},{48,16},{1,33},{17,49},{33,1},{49,17},{2,34}... | collective-permute-start | bytes 13832 | tf_op jit(solution)/shard_map/ppermute | solution.py:32
  60.4 7.9 %collective-permute-start.16 = (bf16[2,160,1536]{2,1,0:T(8,128)(2,1)S(1)}, bf16[2,160,1536]{2,1,0:T(8,128)(2,1)S(1)}, u32[]{:S(2)}, u32[]{:S(2)}) collective-permute-start(bf16[2,160,1536]{2,1,0:T(8,128)(2,1)S(1)} %pad_maximum_fusion.1), channel_id=1, source_target_pairs={{0,64},{64,0},{1,65},{65,1},{2,66},{66,2},{3,67},{67,3},{4,68},{68... | collective-permute-start | bytes 2949128 | tf_op jit(solution)/shard_map/ppermute | solution.py:32
  74.7 4.1 %collective-permute-start.21 = (f32[3,384]{1,0:T(4,128)S(1)}, f32[3,384]{1,0:T(4,128)S(1)}, u32[]{:S(2)}, u32[]{:S(2)}) collective-permute-start(f32[3,384]{1,0:T(4,128)S(1)} %pad_maximum_fusion.32), channel_id=1, source_target_pairs={{0,8},{4,12},{8,0},{12,4},{1,9},{5,13},{9,1},{13,5},{2,10},{6,14},... | collective-permute-start | bytes 13832 | tf_op jit(solution)/shard_map/ppermute | solution.py:32
  87.3 11.9 %collective-permute-start.23 = (bf16[144,1536]{1,0:T(8,128)(2,1)S(1)}, bf16[144,1536]{1,0:T(8,128)(2,1)S(1)}, u32[]{:S(2)}, u32[]{:S(2)}) collective-permute-start(bf16[144,1536]{1,0:T(8,128)(2,1)S(1)} %get-tuple-element.196), channel_id=1, source_target_pairs={{0,4},{4,0},{8,12},{12,8},{1,5},{5,1},{9,13},{13,9},{2,6},{6,2},{1... | collective-permute-start | bytes 1327112 | tf_op jit(solution)/shard_map/ppermute | solution.py:32
  87.4 13.5 %collective-permute-start.25 = (bf16[144,1536]{1,0:T(8,128)(2,1)S(1)}, bf16[144,1536]{1,0:T(8,128)(2,1)S(1)}, u32[]{:S(2)}, u32[]{:S(2)}) collective-permute-start(bf16[144,1536]{1,0:T(8,128)(2,1)S(1)} %get-tuple-element.197), channel_id=1, source_target_pairs={{0,12},{4,8},{8,4},{12,0},{1,13},{5,9},{9,5},{13,1},{2,14},{6,10},... | collective-permute-start | bytes 1327112 | tf_op jit(solution)/shard_map/ppermute | solution.py:32
  88.0 14.5 %collective-permute-start.24 = (bf16[144,1536]{1,0:T(8,128)(2,1)S(1)}, bf16[144,1536]{1,0:T(8,128)(2,1)S(1)}, u32[]{:S(2)}, u32[]{:S(2)}) collective-permute-start(bf16[144,1536]{1,0:T(8,128)(2,1)S(1)} %get-tuple-element.198), channel_id=1, source_target_pairs={{0,8},{4,12},{8,0},{12,4},{1,9},{5,13},{9,1},{13,5},{2,10},{6,14},... | collective-permute-start | bytes 1327112 | tf_op jit(solution)/shard_map/ppermute | solution.py:32
  93.4 36.9 %collective-permute-start.22 = (bf16[2,128,1536]{2,1,0:T(8,128)(2,1)S(1)}, bf16[2,128,1536]{2,1,0:T(8,128)(2,1)S(1)}, u32[]{:S(2)}, u32[]{:S(2)}) collective-permute-start(bf16[2,128,1536]{2,1,0:T(8,128)(2,1)S(1)} %pad_maximum_fusion.2), channel_id=1, source_target_pairs={{0,64},{64,0},{1,65},{65,1},{2,66},{66,2},{3,67},{67,3},{4,68},{68... | collective-permute-start | bytes 2359304 | tf_op jit(solution)/shard_map/ppermute | solution.py:32
  102.9 8.4 %collective-permute-start.28 = (bf16[72,1536]{1,0:T(8,128)(2,1)S(1)}, bf16[72,1536]{1,0:T(8,128)(2,1)S(1)}, u32[]{:S(2)}, u32[]{:S(2)}) collective-permute-start(bf16[72,1536]{1,0:T(8,128)(2,1)S(1)} %get-tuple-element.189), channel_id=1, source_target_pairs={{0,48},{16,32},{32,16},{48,0},{1,49},{17,33},{33,17},{49,1},{2,50}... | collective-permute-start | bytes 663560 | tf_op jit(solution)/shard_map/ppermute | solution.py:32
  105.7 9.9 %collective-permute-start.27 = (bf16[72,1536]{1,0:T(8,128)(2,1)S(1)}, bf16[72,1536]{1,0:T(8,128)(2,1)S(1)}, u32[]{:S(2)}, u32[]{:S(2)}) collective-permute-start(bf16[72,1536]{1,0:T(8,128)(2,1)S(1)} %get-tuple-element.190), channel_id=1, source_target_pairs={{0,32},{16,48},{32,0},{48,16},{1,33},{17,49},{33,1},{49,17},{2,34}... | collective-permute-start | bytes 663560 | tf_op jit(solution)/shard_map/ppermute | solution.py:32
  109.7 17.3 %collective-permute-start.26 = (bf16[72,1536]{1,0:T(8,128)(2,1)S(1)}, bf16[72,1536]{1,0:T(8,128)(2,1)S(1)}, u32[]{:S(2)}, u32[]{:S(2)}) collective-permute-start(bf16[72,1536]{1,0:T(8,128)(2,1)S(1)} %get-tuple-element.191), channel_id=1, source_target_pairs={{0,16},{16,0},{32,48},{48,32},{1,17},{17,1},{33,49},{49,33},{2,18}... | collective-permute-start | bytes 663560 | tf_op jit(solution)/shard_map/ppermute | solution.py:32
  132.4 15.1 %collective-permute-start.32 = (bf16[54,1536]{1,0:T(8,128)(2,1)S(1)}, bf16[54,1536]{1,0:T(8,128)(2,1)S(1)}, u32[]{:S(2)}, u32[]{:S(2)}) collective-permute-start(bf16[54,1536]{1,0:T(8,128)(2,1)S(1)} %get-tuple-element.182), channel_id=1, source_target_pairs={{0,3},{1,2},{2,1},{3,0},{4,7},{5,6},{6,5},{7,4},{8,11},{9,10},{10,... | collective-permute-start | bytes 497672 | tf_op jit(solution)/shard_map/ppermute | solution.py:32
  140.1 7.4 %collective-permute-start.31 = (bf16[54,1536]{1,0:T(8,128)(2,1)S(1)}, bf16[54,1536]{1,0:T(8,128)(2,1)S(1)}, u32[]{:S(2)}, u32[]{:S(2)}) collective-permute-start(bf16[54,1536]{1,0:T(8,128)(2,1)S(1)} %get-tuple-element.183), channel_id=1, source_target_pairs={{0,2},{1,3},{2,0},{3,1},{4,6},{5,7},{6,4},{7,5},{8,10},{9,11},{10,... | collective-permute-start | bytes 497672 | tf_op jit(solution)/shard_map/ppermute | solution.py:32
  140.1 8.2 %collective-permute-start.30 = (bf16[54,1536]{1,0:T(8,128)(2,1)S(1)}, bf16[54,1536]{1,0:T(8,128)(2,1)S(1)}, u32[]{:S(2)}, u32[]{:S(2)}) collective-permute-start(bf16[54,1536]{1,0:T(8,128)(2,1)S(1)} %get-tuple-element.184), channel_id=1, source_target_pairs={{0,1},{1,0},{2,3},{3,2},{4,5},{5,4},{6,7},{7,6},{8,9},{9,8},{10,11... | collective-permute-start | bytes 497672 | tf_op jit(solution)/shard_map/ppermute | solution.py:32
  140.8 15.8 %collective-permute-start.29 = (bf16[128,1536]{1,0:T(8,128)(2,1)S(1)}, bf16[128,1536]{1,0:T(8,128)(2,1)S(1)}, u32[]{:S(2)}, u32[]{:S(2)}) collective-permute-start(bf16[128,1536]{1,0:T(8,128)(2,1)S(1)} %fusion.2), channel_id=1, source_target_pairs={{0,128},{128,0},{1,129},{129,1},{2,130},{130,2},{3,131},{131,3},{4... | collective-permute-start | bytes 1179656 | tf_op jit(solution)/shard_map/ppermute | solution.py:32
  154.9 10.4 %collective-permute-start.34 = (bf16[2,128,384]{2,1,0:T(8,128)(2,1)S(1)}, bf16[2,128,384]{2,1,0:T(8,128)(2,1)S(1)}, u32[]{:S(2)}, u32[]{:S(2)}) collective-permute-start(bf16[2,128,384]{2,1,0:T(8,128)(2,1)S(1)} %pad_maximum_fusion.16), channel_id=1, source_target_pairs={{0,128},{128,0},{1,129},{129,1},{2,130},{130,2},{3,131},{131,3},{4... | collective-permute-start | bytes 589832 | tf_op jit(solution)/shard_map/ppermute | solution.py:32
  155.8 8.2 %collective-permute-start.36 = (f32[33,768]{1,0:T(8,128)S(1)}, f32[33,768]{1,0:T(8,128)S(1)}, u32[]{:S(2)}, u32[]{:S(2)}) collective-permute-start(f32[33,768]{1,0:T(8,128)S(1)} %pad_maximum_fusion.24), channel_id=1, source_target_pairs={{0,128},{128,0},{1,129},{129,1},{2,130},{130,2},{3,131},{131,3},{4... | collective-permute-start | bytes 304136 | tf_op jit(solution)/shard_map/ppermute | solution.py:32
  (24 other events, 209.4 us)
